TPU v7x, 32 devices: a whole 2x2x4 slice. The times are simulated.
32 devices in a mesh: groups: 2 (over y), wide: 4 (over z), narrow: 4 (over x, core).
Axes of the slice: x: 2, y: 2, z: 4, core: 2. Of those that a mesh axis runs over, the one named last changes fastest.
Arguments:
- activations: bfloat16 [2048, 8192], P(('groups', 'wide'), 'narrow'), parts along dimension 0, may hold values from -6 to 6
- request_tenants: int32 [2048, 1], P(('groups', 'wide')), parts along dimension 0, may hold values from 0 to 63; in each aligned block of 256 rows (0 to 255, 256 to 511, ...) at most 16 rows name the same one
- adapter_slot: int32 [64], replicated, may hold values from 0 to 63, each once
- shared_weight: bfloat16 [8192, 2048], P(None, 'narrow'), may hold values from -0.0625 to 0.0625
- adapter_down_weight: bfloat16 [64, 8192, 128], P('wide', 'narrow'), may hold values from -0.0625 to 0.0625
- adapter_up_weight: bfloat16 [64, 64, 2048], P('wide', None, 'narrow'), may hold values from -0.75 to 0.75
Outputs:
- projected: bfloat16 [2048, 2048], P(('groups', 'wide'), 'narrow'), parts along dimension 0
There are 2 independent parts, one for each index of `groups`. A program takes and returns all parts, laid end to end along the dimension named above; an argument that names none is the same for every part. Nothing has to cross between parts.
Inputs may be any that keep to these rules, and one draw needn't show every extreme that they name: `request_tenants`: in each aligned block of 256 rows (the rows of one device) no tenant is named by more than 16 rows, a bound that some block reaches; every tenant is named by some row. `adapter_slot`: A permutation of the tenants.
All inputs are finite; a program needn't handle non-finite values.
Results may differ from a plain program's by a relative error of at most 0.007.
Values may be sent and summed in bfloat16 or wider, within the bound.
No kernel may reach another device: no remote copies, remote signals or barrier semaphores. Data moves between devices by JAX's collectives and lax.ppermute only.
A program may use at most 128 MiB of HBM per device.

v0:
```python
import functools

import jax
import jax.numpy as jnp
from jax import lax
from jax.experimental import pallas as pl
from jax.experimental.pallas import tpu as pltpu
from jax.sharding import PartitionSpec as P

KEY_VALUE_COLS = 1024
LANES = 128
MOST = 16
NEAR = 2
NEAR_ROWS = 112
FAR_ROWS = 96
LATER_ROWS = 32
VMEM = pltpu.VMEM
MIB = 1 << 20

f32, bf16, i32 = jnp.float32, jnp.bfloat16, jnp.int32


def first_turn(wide_size, local_count):
    most = -(-(local_count * MOST + 1) // 32) * 32
    blocks = [(k, 0, min(NEAR_ROWS if k < NEAR else FAR_ROWS, most)) for k in range(wide_size)]
    half = wide_size // 2
    return blocks[1 : half + 1][::-1], blocks[half + 1 :] + blocks[:1]


def ends(blocks, wide_size):
    return [max(start + count - 1 for j, start, count in blocks if j == k) for k in range(wide_size)]


def swap(x, axis, k):
    size = lax.axis_size(axis)
    return lax.ppermute(x, axis, [(i, i ^ k) for i in range(size)])


def after(x, *others):
    return lax.optimization_barrier((x, *others))[0]


def after_all(xs, *others):
    return lax.optimization_barrier((xs, others))[0]


def cost(flops, bytes_accessed, scale=0.001):
    return pl.CostEstimate(
        flops=int(flops * scale), bytes_accessed=int(bytes_accessed * scale), transcendentals=0
    )


def params(mib):
    return pltpu.CompilerParams(vmem_limit_bytes=mib * MIB)


def in_hbm(x):
    return pltpu.with_memory_space_constraint(x, pltpu.HBM)


def pack_kernel(
    local_count, wide_size, layout, span, per_turn, where_ref, tenant_ref, slot_ref, act_ref, *refs
):
    picked = range(*span)
    begun_ref, place_ref = refs[:2]
    blocks = dict(zip(picked, refs[2:-2]))
    act_held, in_sem = refs[-2:]
    rows, features = act_held.shape
    chunks = in_sem.shape[0]
    width = features // chunks

    def load(c):
        cols = pl.ds(c * width, width)
        return pltpu.make_async_copy(act_ref.at[:, cols], act_held.at[:, cols], in_sem.at[c])

    for c in range(chunks):
        load(c).start()
    begun_ref[0, 0] = jnp.int32(1)

    tenants = slot_ref.shape[1]
    tenant = tenant_ref[...]
    named = tenant == lax.broadcasted_iota(i32, (tenants, rows), 0)
    slots = jnp.broadcast_to(slot_ref[...].astype(f32), (8, tenants)).astype(bf16)
    slot = jnp.dot(slots, named.astype(f32).astype(bf16), preferred_element_type=f32)[:1]
    dest = jnp.floor((slot + 0.5) * (1.0 / local_count))
    adapter = slot - dest * local_count + 1.0
    leap = jnp.bitwise_xor(dest.astype(i32), where_ref[0])
    padded = max(8, wide_size)
    goes = (leap == lax.broadcasted_iota(i32, (padded, rows), 0)).astype(f32)
    earlier = lax.broadcasted_iota(i32, (rows, rows), 0) < lax.broadcasted_iota(
        i32, (rows, rows), 1
    )
    before = jnp.dot(
        goes.astype(bf16), earlier.astype(f32).astype(bf16), preferred_element_type=f32
    )
    position = jnp.sum(goes * before, axis=0, keepdims=True).astype(i32)
    adapters = jnp.broadcast_to(adapter, (8, rows)).astype(bf16)
    place = jnp.full((1, rows), -1, i32)
    more = jnp.zeros((1, rows), f32)
    position = position - where_ref[2] * per_turn
    for k, end in enumerate(ends(layout, wide_size)):
        more = jnp.where((leap == k) & (position >= end), 1.0, more)
    offset, here = 0, []
    for k, start, count in layout:
        mine = position - start
        mine = jnp.where((leap == k) & (mine >= 0) & (mine < count - 1), mine, -1)
        place = jnp.where(mine >= 0, mine + offset, place)
        offset += count
        here.append(mine)
    any_more = jnp.max(more, axis=1, keepdims=True)

    for n in picked:
        count = layout[n][2]
        perm = (lax.broadcasted_iota(i32, (count, rows), 0) == here[n]).astype(f32).astype(bf16)
        filler = jnp.zeros((LANES - count, rows), bf16)
        ids = lax.dot_general(
            adapters,
            jnp.concatenate([perm, filler], axis=0),
            (((1,), (1,)), ((), ())),
            preferred_element_type=f32,
        )[:1]
        lane = lax.broadcasted_iota(i32, (1, LANES), 1)
        ids = jnp.where(lane == LANES - 1, any_more, ids)
        last = lax.broadcasted_iota(i32, (count, LANES), 0) == count - 1
        for c in range(chunks):
            cols = pl.ds(c * width, width)
            if n == picked[0]:
                load(c).wait()
            body = jnp.dot(perm, act_held[:, cols], preferred_element_type=f32)
            if c == 0:
                first = jnp.where(last, ids, body[:, :LANES])
                body = jnp.concatenate([first, body[:, LANES:]], axis=1)
            blocks[n][:, cols] = body.astype(bf16)
    place_ref[...] = jnp.broadcast_to(place.astype(f32), (LANES, rows)).T

def pack(where, tenant, slot, activations, local_count, wide_size, layout, span, per_turn):
    rows, features = activations.shape
    counts = [count for _, _, count in layout[slice(*span)]]
    chunks = 4
    whole = pl.BlockSpec(memory_space=VMEM)
    scalar = pl.BlockSpec(memory_space=pltpu.SMEM)
    return pl.pallas_call(
        functools.partial(pack_kernel, local_count, wide_size, layout, span, per_turn),
        out_shape=[
            jax.ShapeDtypeStruct((1, 1), i32),
            jax.ShapeDtypeStruct((rows, LANES), f32),
        ]
        + [pltpu.VMEM((c, features), bf16) for c in counts],
        in_specs=[scalar, whole, whole, pl.BlockSpec(memory_space=pltpu.HBM)],
        out_specs=[scalar, whole] + [whole for _ in counts],
        scratch_shapes=[VMEM((rows, features), bf16), pltpu.SemaphoreType.DMA((chunks,))],
        compiler_params=params(12),
        cost_estimate=cost(2 * sum(counts) * rows * features, 2 * features * (rows + sum(counts))),
        name="pack_rows",
    )(where, tenant, slot, in_hbm(activations))


def stage_kernel(down_ref, up_ref, down_out, up_out, sem):
    adapters, _, width = down_ref.shape
    copies = [
        pltpu.make_async_copy(
            down_ref.at[j], down_out.at[:, pl.ds(j * width, width)], sem.at[j]
        )
        for j in range(adapters)
    ]
    copies.append(pltpu.make_async_copy(up_ref, up_out, sem.at[adapters]))
    for copy in copies:
        copy.start()
    for copy in copies:
        copy.wait()


def stage(down_weight, up_weight):
    adapters, features, width = down_weight.shape
    whole = pl.BlockSpec(memory_space=VMEM)
    return pl.pallas_call(
        stage_kernel,
        out_shape=[
            pltpu.VMEM((features, adapters * width), down_weight.dtype),
            pltpu.VMEM(up_weight.shape, up_weight.dtype),
        ],
        in_specs=[pl.BlockSpec(memory_space=pltpu.HBM)] * 2,
        out_specs=[whole, whole],
        scratch_shapes=[pltpu.SemaphoreType.DMA((adapters + 1,))],
        compiler_params=params(12),
        cost_estimate=cost(10, 10),
        name="stage_maps",
    )(in_hbm(down_weight), in_hbm(up_weight))


def down_kernel(count, cols, narrow_size, per_step, where_ref, *refs):
    xs, weight_ref = refs[:count], refs[count]
    flag_ref, ids_ref = refs[count + 1 : count + 3]
    parts = refs[count + 3 : count + 3 + narrow_size]
    (held_ref,) = refs[count + 3 + narrow_size :]
    steps = weight_ref.shape[1] // (per_step * LANES)

    offsets = [sum(x.shape[0] for x in xs[:n]) for n in range(count)]

    flag = jnp.zeros((1, LANES), f32)
    for n in range(count):
        rows = xs[n].shape[0]
        held_ref[pl.ds(offsets[n], rows), :] = xs[n][...]
        last = held_ref[pl.ds(offsets[n] + rows - 16, 16), :LANES].astype(f32)[15:]
        flag = jnp.maximum(flag, last)
        turned = jnp.broadcast_to(last, (LANES, LANES)).T[:rows]
        keep = lax.broadcasted_iota(i32, (rows, LANES), 0) < rows - 1
        ids_ref[pl.ds(offsets[n], rows), :] = jnp.where(keep, turned, 0.0)
    lane = lax.broadcasted_iota(i32, (1, LANES), 1)
    flag_ref[0, 0] = jnp.max(jnp.where(lane == LANES - 1, flag, 0.0)).astype(i32)

    ids = ids_ref[...]
    total = jnp.zeros(ids.shape, f32)
    for c in range(steps):
        weights = weight_ref[:, c * per_step * LANES : (c + 1) * per_step * LANES]
        found = jnp.dot(held_ref[...], weights, preferred_element_type=f32)
        for j in range(per_step):
            name = c * per_step + j + 1.0
            total = jnp.where(ids == name, found[:, j * LANES : (j + 1) * LANES], total)

    half = total.shape[0] // 2
    rank = LANES // 2
    top, bottom = total[:half], total[half:]
    low = lax.broadcasted_iota(i32, (half, LANES), 1) < rank
    keys = jnp.where(low, top, pltpu.roll(bottom, rank, 1))
    values = jnp.where(low, pltpu.roll(top, rank, 1), bottom)
    for j in range(narrow_size):
        start = jnp.bitwise_xor(where_ref[1], j) * cols
        parts[j][...] = jnp.where(start >= KEY_VALUE_COLS, values, keys).astype(parts[j].dtype)


def down(where, blocks, weight, cols, narrow_size, scale):
    features, width = weight.shape
    rows = sum(b.shape[0] for b in blocks)
    per_step = min(4, width // LANES)
    whole = pl.BlockSpec(memory_space=VMEM)
    scalar = pl.BlockSpec(memory_space=pltpu.SMEM)
    return pl.pallas_call(
        functools.partial(down_kernel, len(blocks), cols, narrow_size, per_step),
        out_shape=[
            jax.ShapeDtypeStruct((1, 1), i32),
            jax.ShapeDtypeStruct((rows, LANES), f32),
        ]
        + [jax.ShapeDtypeStruct((rows // 2, LANES), bf16 if j else f32) for j in range(narrow_size)],
        in_specs=[scalar] + [whole for _ in blocks] + [whole],
        out_specs=[scalar, whole] + [whole for _ in range(narrow_size)],
        scratch_shapes=[VMEM((rows, features), bf16)],
        compiler_params=params(18),
        cost_estimate=cost(2 * rows * features * width, 2 * features * (rows + width), scale),
        name="down_maps",
    )(where, *blocks, weight)


def up_kernel(narrow_size, ids_ref, *refs):
    parts, weight_ref, outs = refs[:narrow_size], refs[narrow_size], refs[narrow_size + 1 :]
    total = parts[0][...]
    for part in parts[1:]:
        total = total + part[...].astype(f32)
    low_rank = total.astype(bf16).astype(f32)
    rank = LANES // 2
    turned = pltpu.roll(low_rank, rank, 1)
    low = lax.broadcasted_iota(i32, low_rank.shape, 1) < rank
    twice = jnp.concatenate(
        [jnp.where(low, low_rank, turned), jnp.where(low, turned, low_rank)], axis=0
    )
    ids = ids_ref[...]
    second = (lax.broadcasted_iota(i32, ids.shape, 1) >= rank).astype(f32)
    adapters = weight_ref.shape[0] // rank
    left = [
        jnp.where(ids - second == 2.0 * pair + 1.0, twice, 0.0).astype(bf16)
        for pair in range(adapters // 2)
    ]
    found = jnp.dot(jnp.concatenate(left, axis=1), weight_ref[...], preferred_element_type=f32)
    offset = 0
    for out in outs:
        rows = out.shape[0]
        out[...] = found[offset : offset + rows].astype(bf16)
        offset += rows


def up(ids, parts, weight, counts):
    cols = weight.shape[1]
    return pl.pallas_call(
        functools.partial(up_kernel, len(parts)),
        out_shape=[jax.ShapeDtypeStruct((c, cols), bf16) for c in counts],
        compiler_params=params(10),
        cost_estimate=cost(2 * sum(counts) * weight.size, 2 * weight.size + 2 * sum(counts) * (cols + 512)),
        name="up_maps",
    )(ids, *parts, weight)


def base_kernel(count, where_ref, *refs):
    acts, weight_ref, so_far, out_ref = refs[:count], refs[count], refs[count + 1 : -1], refs[-1]
    step = pl.program_id(0)
    for j in range(count):

        @pl.when(step == j)
        def _(j=j):
            found = jnp.dot(acts[j][...], weight_ref[...], preferred_element_type=f32)
            if j:
                found = out_ref[...] + found
            elif so_far:
                found = so_far[0][...] + found
            out_ref[...] = found


def base(where, acts, first, weight, so_far):
    rows, features = acts[0].shape
    cols = weight.shape[1]
    count = len(acts)
    given = [] if so_far is None else [so_far]
    return pl.pallas_call(
        functools.partial(base_kernel, count),
        grid_spec=pltpu.PrefetchScalarGridSpec(
            num_scalar_prefetch=1,
            grid=(count,),
            in_specs=[pl.BlockSpec((rows, features), lambda i, where: (0, 0)) for _ in acts]
            + [
                pl.BlockSpec(
                    (features, cols),
                    lambda i, where: (jnp.bitwise_xor(where[1], first + i), 0),
                )
            ]
            + [pl.BlockSpec((rows, cols), lambda i, where: (0, 0)) for _ in given],
            out_specs=pl.BlockSpec((rows, cols), lambda i, where: (0, 0)),
        ),
        out_shape=jax.ShapeDtypeStruct((rows, cols), f32),
        compiler_params=params(14),
        cost_estimate=cost(2 * rows * features * count * cols, 2 * features * count * (cols + rows)),
        name="shared_projection",
    )(where, *acts, in_hbm(weight), *given)


def join_kernel(base_ref, place_ref, *refs):
    corrections, out_ref, held_ref, sem = refs[:-3], *refs[-3:]
    stacked = jnp.concatenate([c[...] for c in corrections], axis=0)
    rows, count = base_ref.shape[0], stacked.shape[0]
    parts = sem.shape[0]
    copies = []
    for n in range(parts):
        part = pl.ds(n * (rows // parts), rows // parts)
        place = place_ref[part, :1].astype(i32)
        perm = lax.broadcasted_iota(i32, (rows // parts, count), 1) == place
        found = jnp.dot(perm.astype(f32).astype(bf16), stacked, preferred_element_type=f32)
        held_ref[part, :] = (base_ref[part, :] + found).astype(out_ref.dtype)
        copy = pltpu.make_async_copy(held_ref.at[part, :], out_ref.at[part, :], sem.at[n])
        copy.start()
        copies.append(copy)
    for copy in copies:
        copy.wait()


def join(base_out, place, corrections, dtype):
    rows, cols = base_out.shape
    count = sum(c.shape[0] for c in corrections)
    parts = 2
    return pl.pallas_call(
        join_kernel,
        out_shape=pltpu.HBM((rows, cols), dtype),
        in_specs=[pl.BlockSpec(memory_space=VMEM)] * (2 + len(corrections)),
        out_specs=pl.BlockSpec(memory_space=pltpu.HBM),
        scratch_shapes=[VMEM((rows, cols), dtype), pltpu.SemaphoreType.DMA((parts,))],
        compiler_params=params(10),
        cost_estimate=cost(2 * rows * cols * count, 2 * cols * (count + 3 * rows)),
        name="join_corrections",
    )(base_out, place, *corrections)


def answers_for(where, blocks, staged, narrow_size, scale=0.001):
    down_weight, up_weight = staged
    more, ids, *parts = down(where, blocks, down_weight, up_weight.shape[1], narrow_size, scale)
    parts = [swap(p, "narrow", j) if j else p for j, p in enumerate(parts)]
    return up(ids, parts, up_weight, [b.shape[0] for b in blocks]), more


def later_turn(turn, axes, total, done, tenant, slot, activations, down_weight, up_weight):
    wide_size, narrow_size = lax.axis_size("wide"), lax.axis_size("narrow")
    where = jnp.stack([*axes, turn])
    layout = [(k, end, LATER_ROWS) for k, end in enumerate(done)]
    _, place, *sent = pack(
        where,
        tenant,
        slot,
        activations,
        down_weight.shape[0],
        wide_size,
        layout,
        (0, wide_size),
        LATER_ROWS - 1,
    )
    got = [swap(b, "wide", k) if k else b for k, b in enumerate(sent)]
    outs, more = answers_for(where, got, stage(down_weight, up_weight), narrow_size)
    answers = [swap(b, "wide", k) if k else b for k, b in enumerate(outs)]
    return join(total, place, answers, f32), more[0, 0]


def on_device(
    activations,
    request_tenants,
    adapter_slot,
    shared_weight,
    adapter_down_weight,
    adapter_up_weight,
):
    rows = activations.shape[0]
    wide_size, narrow_size = lax.axis_size("wide"), lax.axis_size("narrow")
    local_count = adapter_down_weight.shape[0]
    axes = (lax.axis_index("wide").astype(i32), lax.axis_index("narrow").astype(i32))
    where = jnp.stack([*axes, jnp.int32(0)])
    tenant = request_tenants.reshape(1, rows)
    slot = adapter_slot.reshape(1, -1)
    up_weight = adapter_up_weight.reshape(-1, adapter_up_weight.shape[-1])

    cols = up_weight.shape[1]
    first, second = first_turn(wide_size, local_count)
    layout = first + second
    routed = (local_count, wide_size, layout)
    begun, place, *sent = pack(
        where, tenant, slot, activations, *routed, (0, len(first)), 0
    )
    got = [swap(b, "wide", k) for (k, _, _), b in zip(first, sent)]
    half = narrow_size // 2

    def step(work, *operands):
        def never(*operands):
            return jax.tree.map(
                lambda s: jnp.zeros(s.shape, s.dtype), jax.eval_shape(work, *operands)
            )

        return lax.cond(begun[0, 0] > 0, work, never, *operands)

    def spread(act):
        acts, bit = {0: act}, half // 2
        while bit:
            acts.update({j ^ bit: swap(x, "narrow", bit) for j, x in list(acts.items())})
            bit //= 2
        return [acts[j] for j in sorted(acts)]

    def work_before(tenant, slot, activations, shared_weight, maps):
        _, _, *sent = pack(
            where, tenant, slot, activations, *routed, (len(first), len(layout)), 0
        )
        return sent, base(where, spread(activations), 0, shared_weight, None), stage(*maps)

    def work_on_first(blocks, staged, maps):
        outs, more = answers_for(where, blocks, staged, narrow_size)
        return outs, more, stage(*maps)

    def work_on_second(blocks, staged, acts, shared_weight, base_out):
        outs, more = [], jnp.zeros((1, 1), i32)
        if blocks:
            outs, more = answers_for(where, blocks, staged, narrow_size)
            acts = after_all(acts, *outs)
            outs = [swap(b, "wide", k) for (k, _, _), b in zip(second, outs)]
        acts = [x for act in acts for x in spread(act)]
        if acts:
            base_out = base(where, acts, half, shared_weight, base_out)
        return outs, more, base_out

    sent_first = sent
    shared_weight, maps = after_all((shared_weight, (adapter_down_weight, up_weight)), *sent)
    sent, base_out, staged = step(work_before, tenant, slot, activations, shared_weight, maps)
    late = [swap(b, "wide", k) for (k, _, _), b in zip(second, sent[:-1])]
    across = [swap(after(activations, *sent_first), "narrow", half)] if half else []
    outs, more, staged = step(work_on_first, [*got, sent[-1]], staged, maps)
    late = after_all(late, *outs)
    answers = [swap(b, "wide", k) for (k, _, _), b in zip(first, outs)]
    late_answers, late_more, base_out = step(
        work_on_second, late, staged, across, shared_weight, base_out
    )
    answers = [*answers, *late_answers, outs[-1]]
    more = jnp.maximum(more, late_more)
    more = more[0, 0]

    def done(base_out):
        return join(base_out, place, answers, bf16)

    def go_on(base_out):
        def turn_of(state):
            turn, _, total = state
            total, more = later_turn(
                turn, axes, total, ends(layout, wide_size), tenant, slot, activations, adapter_down_weight, up_weight
            )
            return turn + 1, more, total

        state = (jnp.int32(0), jnp.int32(1), join(base_out, place, answers, f32))
        return lax.while_loop(lambda s: s[1] > 0, turn_of, state)[2].astype(bf16)

    return lax.cond(more > 0, go_on, done, base_out)


def solution(mesh):
    in_specs = (
        P(("groups", "wide"), "narrow"),
        P(("groups", "wide"), None),
        P(),
        P(None, "narrow"),
        P("wide", "narrow", None),
        P("wide", None, "narrow"),
    )
    out_specs = P(("groups", "wide"), "narrow")
    return jax.shard_map(
        on_device, mesh=mesh, in_specs=in_specs, out_specs=out_specs, check_vma=False
    )
```

profile of v0, /device:TPU:0, one launch (start us, length us, event | category | flops | bytes accessed | tf_op | source)
XLA Modules:
  0.0 69.3 jit_solution(11499039629445355136)
XLA Ops:
  0.1 3.2 %pack_rows.8 = (s32[1,1]{1,0:T(1,128)}, f32[256,128]{1,0:T(8,128)S(1)}, bf16[96,2048]{1,0:T(8,128)(2,1)}, bf16[112,2048]{1,0:T(8,128)(2,1)S(1)}) custom-call(s32[3]{0:T(128)S(1)} %pad_add_fusion.1.where_ref, s32[1,256]{1,0:T(1,128)} %bitcast.22, s32[1,64]{1,0:T(1,128)} %bitcast.25, bf16[256,2048]{1,0:T(8,128)(2,1)} %act_ref.1), custom_call_target="tpu_custom_call" | custom-call | flops 218103 | bytes 1900 | tf_op jit(solution)/shard_map/pack_rows/pallas_call | solution.py:142
  3.3 3.0 %collective-permute-start.21 = (bf16[256,2048]{1,0:T(8,128)(2,1)}, bf16[256,2048]{1,0:T(8,128)(2,1)}, u32[]{:S(2)}, u32[]{:S(2)}) collective-permute-start(bf16[256,2048]{1,0:T(8,128)(2,1)} %act_ref.1), channel_id=1, source_target_pairs={{0,2},{1,3},{2,0},{3,1},{4,6},{5,7},{6,4},{7,5},{8,10},{9,11},{10,... | collective-permute-start | bytes 3145736 | tf_op jit(solution)/shard_map/ppermute | solution.py:36
  6.3 1.6 %collective-permute-start.19 = (bf16[112,2048]{1,0:T(8,128)(2,1)S(1)}, bf16[112,2048]{1,0:T(8,128)(2,1)}, u32[]{:S(2)}, u32[]{:S(2)}) collective-permute-start(bf16[112,2048]{1,0:T(8,128)(2,1)S(1)} %get-tuple-element.413), channel_id=1, source_target_pairs={{0,4},{4,0},{8,12},{12,8},{1,5},{5,1},{9,13},{13,9},{2,6},{6,2},{1... | collective-permute-start | bytes 1376264 | tf_op jit(solution)/shard_map/ppermute | solution.py:36
  7.9 2.6 %collective-permute-start.18 = (bf16[96,2048]{1,0:T(8,128)(2,1)}, bf16[96,2048]{1,0:T(8,128)(2,1)}, u32[]{:S(2)}, u32[]{:S(2)}) collective-permute-start(bf16[96,2048]{1,0:T(8,128)(2,1)} %get-tuple-element.412), channel_id=1, source_target_pairs={{0,8},{4,12},{8,0},{12,4},{1,9},{5,13},{9,1},{13,5},{2,10},{6,14},... | collective-permute-start | bytes 1179656 | tf_op jit(solution)/shard_map/ppermute | solution.py:36
  11.1 11.0 %conditional.4 = (bf16[96,2048]{1,0:T(8,128)(2,1)S(1)}, bf16[112,2048]{1,0:T(8,128)(2,1)S(1)}, f32[256,512]{1,0:T(8,128)S(1)}, bf16[2048,2048]{1,0:T(8,128)(2,1)S(1)}, bf16[1024,512]{1,0:T(8,128)(2,1)S(1)}) conditional(s32[]{:T(128)} %bitcast.8, () %tuple.62, (s32[3]{0:T(128)S(1)}, s32[1,256]{1,0:T(1,128)}, s32[1,64]{1,0:T(1,128)}, ...), branch_computations={%region_0.0_spmd, %region_1.0_spmd} | conditional | flops 1291844 | bytes 10813492 | solution.py:430
  11.2 3.2 %pack_rows.7 = (s32[1,1]{1,0:T(1,128)}, f32[256,128]{1,0:T(8,128)}, bf16[96,2048]{1,0:T(8,128)(2,1)S(1)}, bf16[112,2048]{1,0:T(8,128)(2,1)S(1)}) custom-call(s32[3]{0:T(128)S(1)} %get-tuple-element.297.where_ref, s32[1,256]{1,0:T(1,128)} %get-tuple-element.298.tenant_ref, s32[1,64]{1,0:T(1,128)} %get-tuple-element.299.slot_ref, ...), custom_call_target="tpu_custom_call" | custom-call | flops 218103 | bytes 1900 | tf_op jit(solution)/shard_map/cond/branch_1_fun/pack_rows/pallas_call | solution.py:142
  14.4 3.9 %stage_maps.5 = (bf16[2048,2048]{1,0:T(8,128)(2,1)S(1)}, bf16[1024,512]{1,0:T(8,128)(2,1)S(1)}) custom-call(bf16[16,2048,128]{2,1,0:T(8,128)(2,1)} %get-tuple-element.304.down_ref, bf16[1024,512]{1,0:T(8,128)(2,1)} %get-tuple-element.305.up_ref), custom_call_target="tpu_custom_call" | custom-call | tf_op jit(solution)/shard_map/cond/branch_1_fun/stage_maps/pallas_call | solution.py:176
  18.3 3.9 %shared_projection.2 = f32[256,512]{1,0:T(8,128)S(1)} custom-call(s32[3]{0:T(128)S(1)} %get-tuple-element.297.where_ref, bf16[256,2048]{1,0:T(8,128)(2,1)} %get-tuple-element.300.act_ref.refs_0_, bf16[256,2048]{1,0:T(8,128)(2,1)S(1)} %collective-permute-done.refs_1_, bf16[8192,512]{1,0:T(8,128)(2,1)} %get-tuple-element.303.refs_2_), custom_call_target="tpu_custom_call" | custom-call | flops 1073741 | bytes 6291 | tf_op jit(solution)/shard_map/cond/branch_1_fun/shared_projection/pallas_call | solution.py:312
  22.4 5.0 %collective-permute-done.18 = bf16[96,2048]{1,0:T(8,128)(2,1)} collective-permute-done((bf16[96,2048]{1,0:T(8,128)(2,1)}, bf16[96,2048]{1,0:T(8,128)(2,1)}, u32[]{:S(2)}, u32[]{:S(2)}) %collective-permute-start.18) | collective-permute-done | bytes 393248 | tf_op jit(solution)/shard_map/ppermute | solution.py:36
  27.4 12.3 %conditional.5 = (bf16[96,512]{1,0:T(8,128)(2,1)S(1)}, bf16[112,512]{1,0:T(8,128)(2,1)}, bf16[112,512]{1,0:T(8,128)(2,1)S(1)}, s32[1,1]{1,0:T(1,128)}, bf16[2048...) conditional(s32[]{:T(128)} %bitcast.8, () %tuple.61, (s32[3]{0:T(128)S(1)}, bf16[96,2048]{1,0:T(8,128)(2,1)}, ...), branch_computations={%region_2.0_spmd, %region_3.0_spmd} | conditional | flops 3019898 | bytes 9764930 | solution.py:430
  27.4 4.6 %down_maps.7 = (s32[1,1]{1,0:T(1,128)}, f32[320,128]{1,0:T(8,128)S(1)}, f32[160,128]{1,0:T(8,128)S(1)}, bf16[160,128]{1,0:T(8,128)(2,1)S(1)}, bf16[160,128]{1,0:...) custom-call(s32[3]{0:T(128)S(1)} %get-tuple-element.308.where_ref, bf16[96,2048]{1,0:T(8,128)(2,1)} %get-tuple-element.309.refs_0_, ...), custom_call_target="tpu_custom_call" | custom-call | flops 2684354 | bytes 9699 | tf_op jit(solution)/shard_map/cond/branch_1_fun/down_maps/pallas_call | solution.py:238
  32.7 1.3 %collective-permute-start.3 = (bf16[160,128]{1,0:T(8,128)(2,1)S(1)}, bf16[160,128]{1,0:T(8,128)(2,1)S(1)}, u32[]{:S(2)}, u32[]{:S(2)}) collective-permute-start(bf16[160,128]{1,0:T(8,128)(2,1)S(1)} %get-tuple-element.317), channel_id=1, source_target_pairs={{0,3},{1,2},{2,1},{3,0},{4,7},{5,6},{6,5},{7,4},{8,11},{9,10},{10,... | collective-permute-start | bytes 122888 | tf_op jit(solution)/shard_map/cond/branch_1_fun/ppermute | solution.py:36
  33.9 3.9 %stage_maps.6 = (bf16[2048,2048]{1,0:T(8,128)(2,1)S(1)}, bf16[1024,512]{1,0:T(8,128)(2,1)S(1)}) custom-call(bf16[16,2048,128]{2,1,0:T(8,128)(2,1)} %get-tuple-element.323.down_ref, bf16[1024,512]{1,0:T(8,128)(2,1)} %get-tuple-element.324.up_ref), custom_call_target="tpu_custom_call" | custom-call | tf_op jit(solution)/shard_map/cond/branch_1_fun/stage_maps/pallas_call | solution.py:176
  37.8 1.2 %up_maps.7 = (bf16[96,512]{1,0:T(8,128)(2,1)S(1)}, bf16[112,512]{1,0:T(8,128)(2,1)}, bf16[112,512]{1,0:T(8,128)(2,1)S(1)}) custom-call(f32[320,128]{1,0:T(8,128)S(1)} %get-tuple-element.313.ids_ref, f32[160,128]{1,0:T(8,128)S(1)} %get-tuple-element.314.refs_0_, bf16[160,128]{1,0:T(8,128)(2,1)S(1)} %collective-permute-done.1.refs_1_, ...), custom_call_target="tpu_custom_call" | custom-call | flops 335544 | bytes 1703 | tf_op jit(solution)/shard_map/cond/branch_1_fun/up_maps/pallas_call | solution.py:283
  39.7 3.6 %collective-permute-start.23 = (bf16[112,512]{1,0:T(8,128)(2,1)}, bf16[112,512]{1,0:T(8,128)(2,1)S(1)}, u32[]{:S(2)}, u32[]{:S(2)}) collective-permute-start(bf16[112,512]{1,0:T(8,128)(2,1)} %get-tuple-element.423), channel_id=1, source_target_pairs={{0,4},{4,0},{8,12},{12,8},{1,5},{5,1},{9,13},{13,9},{2,6},{6,2},{1... | collective-permute-start | bytes 344072 | tf_op jit(solution)/shard_map/ppermute | solution.py:36
  43.3 8.4 %collective-permute-start.22 = (bf16[96,512]{1,0:T(8,128)(2,1)S(1)}, bf16[96,512]{1,0:T(8,128)(2,1)S(1)}, u32[]{:S(2)}, u32[]{:S(2)}) collective-permute-start(bf16[96,512]{1,0:T(8,128)(2,1)S(1)} %get-tuple-element.422), channel_id=1, source_target_pairs={{0,8},{4,12},{8,0},{12,4},{1,9},{5,13},{9,1},{13,5},{2,10},{6,14},... | collective-permute-start | bytes 294920 | tf_op jit(solution)/shard_map/ppermute | solution.py:36
  51.8 15.2 %conditional.6 = (bf16[96,512]{1,0:T(8,128)(2,1)}, s32[1,1]{1,0:T(1,128)}, f32[256,512]{1,0:T(8,128)S(1)}) conditional(s32[]{:T(128)} %bitcast.8, () %tuple.66, (s32[3]{0:T(128)S(1)}, bf16[96,2048]{1,0:T(8,128)(2,1)}, bf16[2048,2048]{1,0:T(8,128)(2,1)S(1)}, bf16[1024,512]{1,0:T(8,128)(2,1)S(1)}, bf16[256,2048]{1,0:T(8,128)(2,1)}, ...), branch_computations={%region_4.0_spmd, %region_5.0_spmd} | conditional | flops 1979710 | bytes 6848697 | solution.py:430
  51.8 3.1 %down_maps.8 = (s32[1,1]{1,0:T(1,128)}, f32[96,128]{1,0:T(8,128)S(1)}, f32[48,128]{1,0:T(8,128)S(1)}, bf16[48,128]{1,0:T(8,128)(2,1)S(1)}, bf16[48,128]{1,0:T(8,128)(2,1)S(1)}, /*index=5*/bf16[48,128]{1,0:T(8,128)(2,1)S(1)}) custom-call(s32[3]{0:T(128)S(1)} %get-tuple-element.327.where_ref, bf16[96,2048]{1,0:T(8,128)(2,1)} %get-tuple-element.328.refs_0_, ...), custom_call_target="tpu_custom_call" | custom-call | flops 805306 | bytes 8781 | tf_op jit(solution)/shard_map/cond/branch_1_fun/down_maps/pallas_call | solution.py:238
  55.6 1.3 %collective-permute-start.6 = (bf16[48,128]{1,0:T(8,128)(2,1)S(1)}, bf16[48,128]{1,0:T(8,128)(2,1)S(1)}, u32[]{:S(2)}, u32[]{:S(2)}) collective-permute-start(bf16[48,128]{1,0:T(8,128)(2,1)S(1)} %get-tuple-element.334), channel_id=1, source_target_pairs={{0,3},{1,2},{2,1},{3,0},{4,7},{5,6},{6,5},{7,4},{8,11},{9,10},{10,... | collective-permute-start | bytes 36872 | tf_op jit(solution)/shard_map/cond/branch_1_fun/ppermute | solution.py:36
  56.8 2.0 %collective-permute-done.5.refs_2_ = bf16[48,128]{1,0:T(8,128)(2,1)S(1)} collective-permute-done((bf16[48,128]{1,0:T(8,128)(2,1)S(1)}, bf16[48,128]{1,0:T(8,128)(2,1)S(1)}, u32[]{:S(2)}, u32[]{:S(2)}) %collective-permute-start.5) | collective-permute-done | bytes 12320 | tf_op jit(solution)/shard_map/cond/branch_1_fun/ppermute | solution.py:36
  59.4 2.8 %collective-permute-done.8.refs_1_ = bf16[256,2048]{1,0:T(8,128)(2,1)S(1)} collective-permute-done((bf16[256,2048]{1,0:T(8,128)(2,1)}, bf16[256,2048]{1,0:T(8,128)(2,1)S(1)}, u32[]{:S(2)}, u32[]{:S(2)}) %collective-permute-start.8) | collective-permute-done | bytes 1048608 | tf_op jit(solution)/shard_map/cond/branch_1_fun/ppermute | solution.py:36
  62.1 3.9 %shared_projection.3 = f32[256,512]{1,0:T(8,128)S(1)} custom-call(s32[3]{0:T(128)S(1)} %get-tuple-element.327.where_ref, bf16[256,2048]{1,0:T(8,128)(2,1)} %get-tuple-element.338.refs_0_, bf16[256,2048]{1,0:T(8,128)(2,1)S(1)} %collective-permute-done.8.refs_1_, bf16[8192,512]{1,0:T(8,128)(2,1)} %get-tuple-element.339.refs_2_, f32[256,512]{1,0:T(8,128)S(1)} %copy-done.3), custom_call_target="tpu_custom_call" | custom-call | flops 1073741 | bytes 6291 | tf_op jit(solution)/shard_map/cond/branch_1_fun/shared_projection/pallas_call | solution.py:312
  67.0 2.1 %conditional.7 = (bf16[256,512]{1,0:T(8,128)(2,1)}) conditional(s32[]{:T(128)} %bitcast.10, (f32[256,512]{1,0:T(8,128)S(1)}, f32[256,128]{1,0:T(8,128)S(1)}, bf16[96,512]{1,0:T(8,128)(2,1)S(1)}, bf16[112,512]{1,0:T(8,128)(2,1)S(1)}, bf16[96,512]{1,0:T(8,128)(2,1)}, /*index=5*/bf16[112,512]{1,0:T(8,128)(2,1)S(1)}) %tuple.70, ...), branch_computations={%region_6.0_spmd, %region_7.0_spmd} | conditional | flops 1615860 | bytes 39663864 | solution.py:489
  67.0 1.9 %join_corrections.7 = bf16[256,512]{1,0:T(8,128)(2,1)} custom-call(f32[256,512]{1,0:T(8,128)S(1)} %get-tuple-element.341.base_ref, f32[256,128]{1,0:T(8,128)S(1)} %get-tuple-element.342.place_ref, bf16[96,512]{1,0:T(8,128)(2,1)S(1)} %get-tuple-element.343.refs_0_, bf16[112,512]{1,0:T(8,128)(2,1)S(1)} %get-tuple-element.344.refs_1_, ...), custom_call_target="tpu_custom_call" | custom-call | flops 109051 | bytes 1212 | tf_op jit(solution)/shard_map/cond/branch_0_fun/join_corrections/pallas_call | solution.py:357
  (30 shorter events, 2.8 us)
Async XLA Ops:
  3.3 48.5 %collective-permute-start.21 = (bf16[256,2048]{1,0:T(8,128)(2,1)}, bf16[256,2048]{1,0:T(8,128)(2,1)}, u32[]{:S(2)}, u32[]{:S(2)}) collective-permute-start(bf16[256,2048]{1,0:T(8,128)(2,1)} %act_ref.1), channel_id=1, source_target_pairs={{0,2},{1,3},{2,0},{3,1},{4,6},{5,7},{6,4},{7,5},{8,10},{9,11},{10,... | collective-permute-start | bytes 3145736 | tf_op jit(solution)/shard_map/ppermute | solution.py:36
  6.3 21.1 %collective-permute-start.19 = (bf16[112,2048]{1,0:T(8,128)(2,1)S(1)}, bf16[112,2048]{1,0:T(8,128)(2,1)}, u32[]{:S(2)}, u32[]{:S(2)}) collective-permute-start(bf16[112,2048]{1,0:T(8,128)(2,1)S(1)} %get-tuple-element.413), channel_id=1, source_target_pairs={{0,4},{4,0},{8,12},{12,8},{1,5},{5,1},{9,13},{13,9},{2,6},{6,2},{1... | collective-permute-start | bytes 1376264 | tf_op jit(solution)/shard_map/ppermute | solution.py:36
  7.9 19.5 %collective-permute-start.18 = (bf16[96,2048]{1,0:T(8,128)(2,1)}, bf16[96,2048]{1,0:T(8,128)(2,1)}, u32[]{:S(2)}, u32[]{:S(2)}) collective-permute-start(bf16[96,2048]{1,0:T(8,128)(2,1)} %get-tuple-element.412), channel_id=1, source_target_pairs={{0,8},{4,12},{8,0},{12,4},{1,9},{5,13},{9,1},{13,5},{2,10},{6,14},... | collective-permute-start | bytes 1179656 | tf_op jit(solution)/shard_map/ppermute | solution.py:36
  11.1 7.1 %collective-permute-start = (bf16[256,2048]{1,0:T(8,128)(2,1)}, bf16[256,2048]{1,0:T(8,128)(2,1)S(1)}, u32[]{:S(2)}, u32[]{:S(2)}) collective-permute-start(bf16[256,2048]{1,0:T(8,128)(2,1)} %get-tuple-element.300.act_ref.refs_0_), channel_id=1, source_target_pairs={{0,1},{1,0},{2,3},{3,2},{4,5},{5,4},{6,7},{7,6},{8,9},{9,8},{10,11... | collective-permute-start | bytes 3145736 | tf_op jit(solution)/shard_map/cond/branch_1_fun/ppermute | solution.py:36
  22.1 5.3 %copy-start.2 = (f32[256,512]{1,0:T(8,128)}, f32[256,512]{1,0:T(8,128)S(1)}, u32[]{:S(2)}) copy-start(f32[256,512]{1,0:T(8,128)S(1)} %get-tuple-element.429) | copy-start | bytes 1572868
  22.2 29.6 %collective-permute-start.20 = (bf16[96,2048]{1,0:T(8,128)(2,1)S(1)}, bf16[96,2048]{1,0:T(8,128)(2,1)}, u32[]{:S(2)}, u32[]{:S(2)}) collective-permute-start(bf16[96,2048]{1,0:T(8,128)(2,1)S(1)} %get-tuple-element.421), channel_id=1, source_target_pairs={{0,12},{4,8},{8,4},{12,0},{1,13},{5,9},{9,5},{13,1},{2,14},{6,10},... | collective-permute-start | bytes 1179656 | tf_op jit(solution)/shard_map/ppermute | solution.py:36
  32.0 5.8 %collective-permute-start.1 = (bf16[160,128]{1,0:T(8,128)(2,1)S(1)}, bf16[160,128]{1,0:T(8,128)(2,1)S(1)}, u32[]{:S(2)}, u32[]{:S(2)}) collective-permute-start(bf16[160,128]{1,0:T(8,128)(2,1)S(1)} %get-tuple-element.315), channel_id=1, source_target_pairs={{0,1},{1,0},{2,3},{3,2},{4,5},{5,4},{6,7},{7,6},{8,9},{9,8},{10,11... | collective-permute-start | bytes 122888 | tf_op jit(solution)/shard_map/cond/branch_1_fun/ppermute | solution.py:36
  32.1 5.7 %collective-permute-start.2 = (bf16[160,128]{1,0:T(8,128)(2,1)S(1)}, bf16[160,128]{1,0:T(8,128)(2,1)S(1)}, u32[]{:S(2)}, u32[]{:S(2)}) collective-permute-start(bf16[160,128]{1,0:T(8,128)(2,1)S(1)} %get-tuple-element.316), channel_id=1, source_target_pairs={{0,2},{1,3},{2,0},{3,1},{4,6},{5,7},{6,4},{7,5},{8,10},{9,11},{10,... | collective-permute-start | bytes 122888 | tf_op jit(solution)/shard_map/cond/branch_1_fun/ppermute | solution.py:36
  32.7 5.2 %collective-permute-start.3 = (bf16[160,128]{1,0:T(8,128)(2,1)S(1)}, bf16[160,128]{1,0:T(8,128)(2,1)S(1)}, u32[]{:S(2)}, u32[]{:S(2)}) collective-permute-start(bf16[160,128]{1,0:T(8,128)(2,1)S(1)} %get-tuple-element.317), channel_id=1, source_target_pairs={{0,3},{1,2},{2,1},{3,0},{4,7},{5,6},{6,5},{7,4},{8,11},{9,10},{10,... | collective-permute-start | bytes 122888 | tf_op jit(solution)/shard_map/cond/branch_1_fun/ppermute | solution.py:36
  39.7 27.3 %collective-permute-start.23 = (bf16[112,512]{1,0:T(8,128)(2,1)}, bf16[112,512]{1,0:T(8,128)(2,1)S(1)}, u32[]{:S(2)}, u32[]{:S(2)}) collective-permute-start(bf16[112,512]{1,0:T(8,128)(2,1)} %get-tuple-element.423), channel_id=1, source_target_pairs={{0,4},{4,0},{8,12},{12,8},{1,5},{5,1},{9,13},{13,9},{2,6},{6,2},{1... | collective-permute-start | bytes 344072 | tf_op jit(solution)/shard_map/ppermute | solution.py:36
  43.3 23.6 %collective-permute-start.22 = (bf16[96,512]{1,0:T(8,128)(2,1)S(1)}, bf16[96,512]{1,0:T(8,128)(2,1)S(1)}, u32[]{:S(2)}, u32[]{:S(2)}) collective-permute-start(bf16[96,512]{1,0:T(8,128)(2,1)S(1)} %get-tuple-element.422), channel_id=1, source_target_pairs={{0,8},{4,12},{8,0},{12,4},{1,9},{5,13},{9,1},{13,5},{2,10},{6,14},... | collective-permute-start | bytes 294920 | tf_op jit(solution)/shard_map/ppermute | solution.py:36
  51.8 15.2 %copy-start.4 = (s32[256,1]{0,1:T(1,128)S(1)}, s32[256,1]{0,1:T(1,128)}, u32[]{:S(2)}) copy-start(s32[256,1]{0,1:T(1,128)} %param.17) | copy-start | bytes 3076
  51.8 15.2 %copy-start.5 = (s32[64]{0:T(128)S(1)}, s32[64]{0:T(128)}, u32[]{:S(2)}) copy-start(s32[64]{0:T(128)} %param.18) | copy-start | bytes 772
  51.8 10.3 %copy-start.3 = (f32[256,512]{1,0:T(8,128)S(1)}, f32[256,512]{1,0:T(8,128)}, u32[]{:S(2)}) copy-start(f32[256,512]{1,0:T(8,128)} %get-tuple-element.340.refs_3_) | copy-start | bytes 1572868 | tf_op jit(solution)/shard_map/cond
  54.9 1.9 %collective-permute-start.4 = (bf16[48,128]{1,0:T(8,128)(2,1)S(1)}, bf16[48,128]{1,0:T(8,128)(2,1)S(1)}, u32[]{:S(2)}, u32[]{:S(2)}) collective-permute-start(bf16[48,128]{1,0:T(8,128)(2,1)S(1)} %get-tuple-element.332), channel_id=1, source_target_pairs={{0,1},{1,0},{2,3},{3,2},{4,5},{5,4},{6,7},{7,6},{8,9},{9,8},{10,11... | collective-permute-start | bytes 36872 | tf_op jit(solution)/shard_map/cond/branch_1_fun/ppermute | solution.py:36
  55.0 3.9 %collective-permute-start.5 = (bf16[48,128]{1,0:T(8,128)(2,1)S(1)}, bf16[48,128]{1,0:T(8,128)(2,1)S(1)}, u32[]{:S(2)}, u32[]{:S(2)}) collective-permute-start(bf16[48,128]{1,0:T(8,128)(2,1)S(1)} %get-tuple-element.333), channel_id=1, source_target_pairs={{0,2},{1,3},{2,0},{3,1},{4,6},{5,7},{6,4},{7,5},{8,10},{9,11},{10,... | collective-permute-start | bytes 36872 | tf_op jit(solution)/shard_map/cond/branch_1_fun/ppermute | solution.py:36
  55.6 3.3 %collective-permute-start.6 = (bf16[48,128]{1,0:T(8,128)(2,1)S(1)}, bf16[48,128]{1,0:T(8,128)(2,1)S(1)}, u32[]{:S(2)}, u32[]{:S(2)}) collective-permute-start(bf16[48,128]{1,0:T(8,128)(2,1)S(1)} %get-tuple-element.334), channel_id=1, source_target_pairs={{0,3},{1,2},{2,1},{3,0},{4,7},{5,6},{6,5},{7,4},{8,11},{9,10},{10,... | collective-permute-start | bytes 36872 | tf_op jit(solution)/shard_map/cond/branch_1_fun/ppermute | solution.py:36
  59.2 2.9 %collective-permute-start.8 = (bf16[256,2048]{1,0:T(8,128)(2,1)}, bf16[256,2048]{1,0:T(8,128)(2,1)S(1)}, u32[]{:S(2)}, u32[]{:S(2)}) collective-permute-start(bf16[256,2048]{1,0:T(8,128)(2,1)} %get-tuple-element.338.refs_0_), channel_id=1, source_target_pairs={{0,1},{1,0},{2,3},{3,2},{4,5},{5,4},{6,7},{7,6},{8,9},{9,8},{10,11... | collective-permute-start | bytes 3145736 | tf_op jit(solution)/shard_map/cond/branch_1_fun/ppermute | solution.py:36
  59.4 7.0 %collective-permute-start.7 = (bf16[96,512]{1,0:T(8,128)(2,1)S(1)}, bf16[96,512]{1,0:T(8,128)(2,1)}, u32[]{:S(2)}, u32[]{:S(2)}) collective-permute-start(bf16[96,512]{1,0:T(8,128)(2,1)S(1)} %up_maps.8), channel_id=1, source_target_pairs={{0,12},{4,8},{8,4},{12,0},{1,13},{5,9},{9,5},{13,1},{2,14},{6,10},... | collective-permute-start | bytes 294920 | tf_op jit(solution)/shard_map/cond/branch_1_fun/ppermute | solution.py:36
where the time goes:
time: 69.6 us; the launch traced here: 69.3 us
  Pallas kernels  32.9 us (47%)
  starting transfers between devices  23.6 us (34%)
  waiting for transfers between devices  10.1 us (15%)
  loops' own time  1.61 us (2%)
  between operations  0.91 us (1%)
    ppermute x15, starting transfers between devices, swap(): return lax.ppermute(x, axis, [(i, i ^ k) for i in range(size)])  23.6 us
    ppermute x15, waiting for transfers between devices, swap(): return lax.ppermute(x, axis, [(i, i ^ k) for i in range(size)])  10.1 us
    pallas_call x2, Pallas kernels, base(): pl.pallas_call(functools.partial(base_kernel, count), grid_spec=pltpu.Pre...  7.73 us
    pallas_call x2, Pallas kernels, stage(): pl.pallas_call(stage_kernel, out_shape=[pltpu.VMEM((features, adapters *...  7.73 us
    pallas_call x2, Pallas kernels, down(): pl.pallas_call(functools.partial(down_kernel, len(blocks), cols, narrow_s...  7.65 us
    pallas_call x2, Pallas kernels, pack(): pl.pallas_call(functools.partial(pack_kernel, local_count, wide_size, lay...  6.37 us
    pallas_call x1, Pallas kernels, join(): pl.pallas_call(join_kernel, out_shape=pltpu.HBM((rows, cols), dtype), in_...  1.93 us
    pallas_call x2, Pallas kernels, up(): pl.pallas_call(functools.partial(up_kernel, len(parts)), out_shape=[jax.S...  1.52 us
  transfers between devices with their start and end apart: 15, of which 4 were waited for; matrix products, arithmetic and copies ran while one was open for 0% of the time, Pallas kernels for 40%

commit v1 on v0

--- a/solution.py
+++ b/solution.py
@@ -366,11 +366,15 @@
     )(base_out, place, *corrections)
 
 
-def answers_for(where, blocks, staged, narrow_size, scale=0.001):
-    down_weight, up_weight = staged
-    more, ids, *parts = down(where, blocks, down_weight, up_weight.shape[1], narrow_size, scale)
+def raise_parts(ids, parts, up_weight, counts):
     parts = [swap(p, "narrow", j) if j else p for j, p in enumerate(parts)]
-    return up(ids, parts, up_weight, [b.shape[0] for b in blocks]), more
+    return up(ids, parts, up_weight, counts)
+
+
+def answers_for(where, blocks, maps, narrow_size):
+    down_weight, up_weight = maps
+    more, ids, *parts = down(where, blocks, down_weight, up_weight.shape[1], narrow_size, 0.001)
+    return raise_parts(ids, parts, up_weight, [b.shape[0] for b in blocks]), more
 
 
 def later_turn(turn, axes, total, done, tenant, slot, activations, down_weight, up_weight):
@@ -442,34 +446,32 @@
         )
         return sent, base(where, spread(activations), 0, shared_weight, None), stage(*maps)
 
-    def work_on_first(blocks, staged, maps):
-        outs, more = answers_for(where, blocks, staged, narrow_size)
-        return outs, more, stage(*maps)
-
-    def work_on_second(blocks, staged, acts, shared_weight, base_out):
-        outs, more = [], jnp.zeros((1, 1), i32)
-        if blocks:
-            outs, more = answers_for(where, blocks, staged, narrow_size)
-            acts = after_all(acts, *outs)
-            outs = [swap(b, "wide", k) for (k, _, _), b in zip(second, outs)]
-        acts = [x for act in acts for x in spread(act)]
-        if acts:
-            base_out = base(where, acts, half, shared_weight, base_out)
-        return outs, more, base_out
-
-    sent_first = sent
+    def work_on_first(ids, parts, up_weight, maps):
+        counts = [count for _, _, count in [*first, layout[-1]]]
+        return raise_parts(ids, parts, up_weight, counts), stage(*maps)
+
+    def work_on_second(blocks, maps):
+        return answers_for(where, blocks, maps, narrow_size)
+
+    def work_after(across, shared_weight, base_out):
+        return base(where, spread(across), half, shared_weight, base_out)
+
     shared_weight, maps = after_all((shared_weight, (adapter_down_weight, up_weight)), *sent)
     sent, base_out, staged = step(work_before, tenant, slot, activations, shared_weight, maps)
+    across = swap(after(activations, base_out), "narrow", half) if half else None
     late = [swap(b, "wide", k) for (k, _, _), b in zip(second, sent[:-1])]
-    across = [swap(after(activations, *sent_first), "narrow", half)] if half else []
-    outs, more, staged = step(work_on_first, [*got, sent[-1]], staged, maps)
-    late = after_all(late, *outs)
-    answers = [swap(b, "wide", k) for (k, _, _), b in zip(first, outs)]
-    late_answers, late_more, base_out = step(
-        work_on_second, late, staged, across, shared_weight, base_out
-    )
-    answers = [*answers, *late_answers, outs[-1]]
-    more = jnp.maximum(more, late_more)
+    more, ids, *parts = down(
+        where, [*got, sent[-1]], staged[0], up_weight.shape[1], narrow_size, 20
+    )
+    outs, staged = step(work_on_first, ids, parts, staged[1], maps)
+    if late:
+        late_outs, late_more = step(work_on_second, after_all(late, *outs), staged)
+        more = jnp.maximum(more, late_more)
+        outs = after_all(outs, *late_outs)
+        outs = [*outs[:-1], *late_outs, outs[-1]]
+    answers = [swap(b, "wide", k) if k else b for (k, _, _), b in zip(layout, outs)]
+    if half:
+        base_out = step(work_after, *after_all((across, shared_weight, base_out), *outs))
     more = more[0, 0]
 
     def done(base_out):

time: 69.6 us -> 71.9 us (1.033)
  waiting for transfers between devices: 10.1 us -> 21.7 us
  starting transfers between devices: 23.6 us -> 15.9 us
  Pallas kernels: 32.9 us -> 31.5 us
    ppermute x15, waiting for transfers between devices: 10.1 us -> 21.7 us  [swap(): return lax.ppermute(x, axis, [(i, i ^ k) for i in range(size)])]
    ppermute x15, starting transfers between devices: 23.6 us -> 15.9 us  [swap(): return lax.ppermute(x, axis, [(i, i ^ k) for i in range(size)])]
    pallas_call x1, Pallas kernels: 1.93 us -> 1.04 us  [join(): pl.pallas_call(join_kernel, out_shape=pltpu.HBM((rows, cols), dtype), in_...]
  transfers between devices with their start and end apart: 15 -> 15, of which waited for: 4 -> 7; matrix products, arithmetic and copies ran while one was open for 0% -> 0% of each run, Pallas kernels for 40% -> 38%
where the time goes in v1:
time: 71.9 us; the launch traced here: 71.7 us
  Pallas kernels  31.5 us (44%)
  waiting for transfers between devices  21.7 us (30%)
  starting transfers between devices  15.9 us (22%)
  between operations  1.57 us (2%)
  loops' own time  0.91 us (1%)
    ppermute x15, waiting for transfers between devices, swap(): return lax.ppermute(x, axis, [(i, i ^ k) for i in range(size)])  21.7 us
    ppermute x15, starting transfers between devices, swap(): return lax.ppermute(x, axis, [(i, i ^ k) for i in range(size)])  15.9 us
    pallas_call x2, Pallas kernels, base(): pl.pallas_call(functools.partial(base_kernel, count), grid_spec=pltpu.Pre...  7.74 us
    pallas_call x2, Pallas kernels, stage(): pl.pallas_call(stage_kernel, out_shape=[pltpu.VMEM((features, adapters *...  7.73 us
    pallas_call x2, Pallas kernels, down(): pl.pallas_call(functools.partial(down_kernel, len(blocks), cols, narrow_s...  7.06 us
    pallas_call x2, Pallas kernels, pack(): pl.pallas_call(functools.partial(pack_kernel, local_count, wide_size, lay...  6.39 us
    pallas_call x2, Pallas kernels, up(): pl.pallas_call(functools.partial(up_kernel, len(parts)), out_shape=[jax.S...  1.53 us
  transfers between devices with their start and end apart: 15, of which 7 were waited for; matrix products, arithmetic and copies ran while one was open for 0% of the time, Pallas kernels for 38%

profile of v1, /device:TPU:0, one launch (start us, length us, event | category | flops | bytes accessed | tf_op | source)
XLA Modules:
  0.0 71.7 jit_solution(17214803130854601175)
XLA Ops:
  0.1 3.2 %pack_rows.8 = (s32[1,1]{1,0:T(1,128)}, f32[256,128]{1,0:T(8,128)S(1)}, bf16[96,2048]{1,0:T(8,128)(2,1)}, bf16[112,2048]{1,0:T(8,128)(2,1)S(1)}) custom-call(s32[3]{0:T(128)S(1)} %pad_add_fusion.1.where_ref, s32[1,256]{1,0:T(1,128)} %bitcast.22, s32[1,64]{1,0:T(1,128)} %bitcast.25, bf16[256,2048]{1,0:T(8,128)(2,1)} %act_ref.1), custom_call_target="tpu_custom_call" | custom-call | flops 218103 | bytes 1900 | tf_op jit(solution)/shard_map/pack_rows/pallas_call | solution.py:142
  3.3 3.1 %collective-permute-start.18 = (bf16[112,2048]{1,0:T(8,128)(2,1)S(1)}, bf16[112,2048]{1,0:T(8,128)(2,1)S(1)}, u32[]{:S(2)}, u32[]{:S(2)}) collective-permute-start(bf16[112,2048]{1,0:T(8,128)(2,1)S(1)} %get-tuple-element.421), channel_id=1, source_target_pairs={{0,4},{4,0},{8,12},{12,8},{1,5},{5,1},{9,13},{13,9},{2,6},{6,2},{1... | collective-permute-start | bytes 1376264 | tf_op jit(solution)/shard_map/ppermute | solution.py:36
  6.4 2.6 %collective-permute-start.17 = (bf16[96,2048]{1,0:T(8,128)(2,1)}, bf16[96,2048]{1,0:T(8,128)(2,1)S(1)}, u32[]{:S(2)}, u32[]{:S(2)}) collective-permute-start(bf16[96,2048]{1,0:T(8,128)(2,1)} %get-tuple-element.420), channel_id=1, source_target_pairs={{0,8},{4,12},{8,0},{12,4},{1,9},{5,13},{9,1},{13,5},{2,10},{6,14},... | collective-permute-start | bytes 1179656 | tf_op jit(solution)/shard_map/ppermute | solution.py:36
  9.6 11.1 %conditional.5 = (bf16[96,2048]{1,0:T(8,128)(2,1)S(1)}, bf16[112,2048]{1,0:T(8,128)(2,1)S(1)}, f32[256,512]{1,0:T(8,128)S(1)}, bf16[2048,2048]{1,0:T(8,128)(2,1)S(1)}, bf16[1024,512]{1,0:T(8,128)(2,1)S(1)}) conditional(s32[]{:T(128)} %bitcast.8, () %tuple.68, (s32[3]{0:T(128)S(1)}, s32[1,256]{1,0:T(1,128)}, s32[1,64]{1,0:T(1,128)}, ...), branch_computations={%region_0.0_spmd, %region_1.0_spmd} | conditional | flops 1291844 | bytes 10813492 | solution.py:434
  9.7 3.2 %pack_rows.7 = (s32[1,1]{1,0:T(1,128)}, f32[256,128]{1,0:T(8,128)}, bf16[96,2048]{1,0:T(8,128)(2,1)S(1)}, bf16[112,2048]{1,0:T(8,128)(2,1)S(1)}) custom-call(s32[3]{0:T(128)S(1)} %get-tuple-element.302.where_ref, s32[1,256]{1,0:T(1,128)} %get-tuple-element.303.tenant_ref, s32[1,64]{1,0:T(1,128)} %get-tuple-element.304.slot_ref, ...), custom_call_target="tpu_custom_call" | custom-call | flops 218103 | bytes 1900 | tf_op jit(solution)/shard_map/cond/branch_1_fun/pack_rows/pallas_call | solution.py:142
  12.9 3.9 %stage_maps.5 = (bf16[2048,2048]{1,0:T(8,128)(2,1)S(1)}, bf16[1024,512]{1,0:T(8,128)(2,1)S(1)}) custom-call(bf16[16,2048,128]{2,1,0:T(8,128)(2,1)} %get-tuple-element.309.down_ref, bf16[1024,512]{1,0:T(8,128)(2,1)} %get-tuple-element.310.up_ref), custom_call_target="tpu_custom_call" | custom-call | tf_op jit(solution)/shard_map/cond/branch_1_fun/stage_maps/pallas_call | solution.py:176
  16.8 3.9 %shared_projection.2 = f32[256,512]{1,0:T(8,128)S(1)} custom-call(s32[3]{0:T(128)S(1)} %get-tuple-element.302.where_ref, bf16[256,2048]{1,0:T(8,128)(2,1)} %get-tuple-element.305.act_ref.refs_0_, bf16[256,2048]{1,0:T(8,128)(2,1)S(1)} %collective-permute-done.refs_1_, bf16[8192,512]{1,0:T(8,128)(2,1)} %get-tuple-element.308.refs_2_), custom_call_target="tpu_custom_call" | custom-call | flops 1073741 | bytes 6291 | tf_op jit(solution)/shard_map/cond/branch_1_fun/shared_projection/pallas_call | solution.py:312
  20.8 1.7 %collective-permute-start.20 = (bf16[256,2048]{1,0:T(8,128)(2,1)}, bf16[256,2048]{1,0:T(8,128)(2,1)}, u32[]{:S(2)}, u32[]{:S(2)}) collective-permute-start(bf16[256,2048]{1,0:T(8,128)(2,1)} %act_ref.1), channel_id=1, source_target_pairs={{0,2},{1,3},{2,0},{3,1},{4,6},{5,7},{6,4},{7,5},{8,10},{9,11},{10,... | collective-permute-start | bytes 3145736 | tf_op jit(solution)/shard_map/ppermute | solution.py:36
  22.5 3.4 %collective-permute-done.17.refs_0_ = bf16[96,2048]{1,0:T(8,128)(2,1)S(1)} collective-permute-done((bf16[96,2048]{1,0:T(8,128)(2,1)}, bf16[96,2048]{1,0:T(8,128)(2,1)S(1)}, u32[]{:S(2)}, u32[]{:S(2)}) %collective-permute-start.17) | collective-permute-done | bytes 393248 | tf_op jit(solution)/shard_map/ppermute | solution.py:36
  25.9 4.0 %down_maps.8 = (s32[1,1]{1,0:T(1,128)}, f32[320,128]{1,0:T(8,128)S(1)}, f32[160,128]{1,0:T(8,128)S(1)}, bf16[160,128]{1,0:T(8,128)(2,1)S(1)}, bf16[160,128]{1,0:...) custom-call(s32[3]{0:T(128)S(1)} %pad_add_fusion.1.where_ref, bf16[96,2048]{1,0:T(8,128)(2,1)S(1)} %collective-permute-done.17.refs_0_, ...), custom_call_target="tpu_custom_call" | custom-call | flops 53687091200 | bytes 193986560 | tf_op jit(solution)/shard_map/down_maps/pallas_call | solution.py:238
  29.9 19.2 %conditional.6 = (bf16[96,512]{1,0:T(8,128)(2,1)}, bf16[112,512]{1,0:T(8,128)(2,1)}, bf16[112,512]{1,0:T(8,128)(2,1)S(1)}, bf16[2048,2048]{1,0:T(8,128)(2,1)S(1)}, bf16[1024,512]{1,0:T(8,128)(2,1)S(1)}) conditional(s32[]{:T(128)} %bitcast.8, () %tuple.72, (bf16[160,128]{1,0:T(8,128)(2,1)S(1)}, bf16[160,128]{1,0:T(8,128)(2,1)S(1)}, ...), branch_computations={%region_2.0_spmd, %region_3.0_spmd} | conditional | flops 335544 | bytes 9764914 | solution.py:434
  30.0 1.6 %collective-permute-start.2 = (bf16[160,128]{1,0:T(8,128)(2,1)S(1)}, bf16[160,128]{1,0:T(8,128)(2,1)S(1)}, u32[]{:S(2)}, u32[]{:S(2)}) collective-permute-start(bf16[160,128]{1,0:T(8,128)(2,1)S(1)} %get-tuple-element.316), channel_id=1, source_target_pairs={{0,2},{1,3},{2,0},{3,1},{4,6},{5,7},{6,4},{7,5},{8,10},{9,11},{10,... | collective-permute-start | bytes 122888 | tf_op jit(solution)/shard_map/cond/branch_1_fun/ppermute | solution.py:36
  31.9 3.9 %stage_maps.6 = (bf16[2048,2048]{1,0:T(8,128)(2,1)S(1)}, bf16[1024,512]{1,0:T(8,128)(2,1)S(1)}) custom-call(bf16[16,2048,128]{2,1,0:T(8,128)(2,1)} %get-tuple-element.322.down_ref, bf16[1024,512]{1,0:T(8,128)(2,1)} %get-tuple-element.323.up_ref), custom_call_target="tpu_custom_call" | custom-call | tf_op jit(solution)/shard_map/cond/branch_1_fun/stage_maps/pallas_call | solution.py:176
  35.7 12.1 %collective-permute-done.2.refs_2_ = bf16[160,128]{1,0:T(8,128)(2,1)S(1)} collective-permute-done((bf16[160,128]{1,0:T(8,128)(2,1)S(1)}, bf16[160,128]{1,0:T(8,128)(2,1)S(1)}, u32[]{:S(2)}, u32[]{:S(2)}) %collective-permute-start.2) | collective-permute-done | bytes 40992 | tf_op jit(solution)/shard_map/cond/branch_1_fun/ppermute | solution.py:36
  47.9 1.2 %up_maps.7 = (bf16[96,512]{1,0:T(8,128)(2,1)}, bf16[112,512]{1,0:T(8,128)(2,1)}, bf16[112,512]{1,0:T(8,128)(2,1)S(1)}) custom-call(f32[320,128]{1,0:T(8,128)S(1)} %get-tuple-element.313.ids_ref, f32[160,128]{1,0:T(8,128)S(1)} %get-tuple-element.314.refs_0_, bf16[160,128]{1,0:T(8,128)(2,1)S(1)} %collective-permute-done.1.refs_1_, ...), custom_call_target="tpu_custom_call" | custom-call | flops 335544 | bytes 1703 | tf_op jit(solution)/shard_map/cond/branch_1_fun/up_maps/pallas_call | solution.py:283
  49.1 8.9 %conditional.7 = (bf16[96,512]{1,0:T(8,128)(2,1)S(1)}, s32[1,1]{1,0:T(1,128)}) conditional(s32[]{:T(128)} %bitcast.8, () %tuple.71, (s32[3]{0:T(128)S(1)}, bf16[96,2048]{1,0:T(8,128)(2,1)}, bf16[2048,2048]{1,0:T(8,128)(2,1)S(1)}, bf16[1024,512]{1,0:T(8,128)(2,1)S(1)}) %tuple.75), branch_computations={%region_4.0_spmd, %region_5.0_spmd} | conditional | flops 905969 | bytes 157618 | solution.py:434
  49.1 3.1 %down_maps.7 = (s32[1,1]{1,0:T(1,128)}, f32[96,128]{1,0:T(8,128)S(1)}, f32[48,128]{1,0:T(8,128)S(1)}, bf16[48,128]{1,0:T(8,128)(2,1)S(1)}, bf16[48,128]{1,0:T(8,128)(2,1)S(1)}, /*index=5*/bf16[48,128]{1,0:T(8,128)(2,1)S(1)}) custom-call(s32[3]{0:T(128)S(1)} %get-tuple-element.326.where_ref, bf16[96,2048]{1,0:T(8,128)(2,1)} %get-tuple-element.327.refs_0_, ...), custom_call_target="tpu_custom_call" | custom-call | flops 805306 | bytes 8781 | tf_op jit(solution)/shard_map/cond/branch_1_fun/down_maps/pallas_call | solution.py:238
  52.5 1.5 %collective-permute-start.5 = (bf16[48,128]{1,0:T(8,128)(2,1)S(1)}, bf16[48,128]{1,0:T(8,128)(2,1)S(1)}, u32[]{:S(2)}, u32[]{:S(2)}) collective-permute-start(bf16[48,128]{1,0:T(8,128)(2,1)S(1)} %get-tuple-element.332), channel_id=1, source_target_pairs={{0,2},{1,3},{2,0},{3,1},{4,6},{5,7},{6,4},{7,5},{8,10},{9,11},{10,... | collective-permute-start | bytes 36872 | tf_op jit(solution)/shard_map/cond/branch_1_fun/ppermute | solution.py:36
  54.1 2.1 %collective-permute-done.5.refs_2_ = bf16[48,128]{1,0:T(8,128)(2,1)S(1)} collective-permute-done((bf16[48,128]{1,0:T(8,128)(2,1)S(1)}, bf16[48,128]{1,0:T(8,128)(2,1)S(1)}, u32[]{:S(2)}, u32[]{:S(2)}) %collective-permute-start.5) | collective-permute-done | bytes 12320 | tf_op jit(solution)/shard_map/cond/branch_1_fun/ppermute | solution.py:36
  58.7 3.5 %collective-permute-start.21 = (bf16[96,512]{1,0:T(8,128)(2,1)}, bf16[96,512]{1,0:T(8,128)(2,1)S(1)}, u32[]{:S(2)}, u32[]{:S(2)}) collective-permute-start(bf16[96,512]{1,0:T(8,128)(2,1)} %get-tuple-element.446), channel_id=1, source_target_pairs={{0,8},{4,12},{8,0},{12,4},{1,9},{5,13},{9,1},{13,5},{2,10},{6,14},... | collective-permute-start | bytes 294920 | tf_op jit(solution)/shard_map/ppermute | solution.py:36
  63.2 6.8 %conditional.8 = (f32[256,512]{1,0:T(8,128)S(1)}) conditional(s32[]{:T(128)} %bitcast.8, () %tuple.76, (bf16[256,2048]{1,0:T(8,128)(2,1)}, s32[3]{0:T(128)S(1)}, bf16[8192,512]{1,0:T(8,128)(2,1)}, f32[256,512]{1,0:T(8,128)S(1)}) %tuple.110), branch_computations={%region_6.0_spmd, %region_7.0_spmd} | conditional | flops 1073741 | bytes 4200643 | solution.py:434
  63.3 2.9 %collective-permute-done.7.refs_1_ = bf16[256,2048]{1,0:T(8,128)(2,1)S(1)} collective-permute-done((bf16[256,2048]{1,0:T(8,128)(2,1)}, bf16[256,2048]{1,0:T(8,128)(2,1)S(1)}, u32[]{:S(2)}, u32[]{:S(2)}) %collective-permute-start.7) | collective-permute-done | bytes 1048608 | tf_op jit(solution)/shard_map/cond/branch_1_fun/ppermute | solution.py:36
  66.1 3.9 %shared_projection.3 = f32[256,512]{1,0:T(8,128)S(1)} custom-call(s32[3]{0:T(128)S(1)} %get-tuple-element.336.where_ref, bf16[256,2048]{1,0:T(8,128)(2,1)} %get-tuple-element.337.refs_0_, bf16[256,2048]{1,0:T(8,128)(2,1)S(1)} %collective-permute-done.7.refs_1_, bf16[8192,512]{1,0:T(8,128)(2,1)} %get-tuple-element.338.refs_2_, ...), custom_call_target="tpu_custom_call" | custom-call | flops 1073741 | bytes 6291 | tf_op jit(solution)/shard_map/cond/branch_1_fun/shared_projection/pallas_call | solution.py:312
  70.3 1.2 %conditional.9 = (bf16[256,512]{1,0:T(8,128)(2,1)}) conditional(s32[]{:T(128)} %bitcast.10, (f32[256,512]{1,0:T(8,128)S(1)}, f32[256,128]{1,0:T(8,128)S(1)}, bf16[96,512]{1,0:T(8,128)(2,1)S(1)}, bf16[112,512]{1,0:T(8,128)(2,1)S(1)}, bf16[96,512]{1,0:T(8,128)(2,1)S(1)}, /*index=5*/bf16[112,512]{1,0:T(8,128)(2,1)S(1)}) %tuple.81, ...), branch_computations={%region_8.0_spmd, %region_9.0_spmd} | conditional | flops 1615860 | bytes 39663864 | solution.py:491
  (31 shorter events, 4.7 us)
Async XLA Ops:
  3.3 22.6 %collective-permute-start.18 = (bf16[112,2048]{1,0:T(8,128)(2,1)S(1)}, bf16[112,2048]{1,0:T(8,128)(2,1)S(1)}, u32[]{:S(2)}, u32[]{:S(2)}) collective-permute-start(bf16[112,2048]{1,0:T(8,128)(2,1)S(1)} %get-tuple-element.421), channel_id=1, source_target_pairs={{0,4},{4,0},{8,12},{12,8},{1,5},{5,1},{9,13},{13,9},{2,6},{6,2},{1... | collective-permute-start | bytes 1376264 | tf_op jit(solution)/shard_map/ppermute | solution.py:36
  6.4 19.5 %collective-permute-start.17 = (bf16[96,2048]{1,0:T(8,128)(2,1)}, bf16[96,2048]{1,0:T(8,128)(2,1)S(1)}, u32[]{:S(2)}, u32[]{:S(2)}) collective-permute-start(bf16[96,2048]{1,0:T(8,128)(2,1)} %get-tuple-element.420), channel_id=1, source_target_pairs={{0,8},{4,12},{8,0},{12,4},{1,9},{5,13},{9,1},{13,5},{2,10},{6,14},... | collective-permute-start | bytes 1179656 | tf_op jit(solution)/shard_map/ppermute | solution.py:36
  9.6 7.2 %collective-permute-start = (bf16[256,2048]{1,0:T(8,128)(2,1)}, bf16[256,2048]{1,0:T(8,128)(2,1)S(1)}, u32[]{:S(2)}, u32[]{:S(2)}) collective-permute-start(bf16[256,2048]{1,0:T(8,128)(2,1)} %get-tuple-element.305.act_ref.refs_0_), channel_id=1, source_target_pairs={{0,1},{1,0},{2,3},{3,2},{4,5},{5,4},{6,7},{7,6},{8,9},{9,8},{10,11... | collective-permute-start | bytes 3145736 | tf_op jit(solution)/shard_map/cond/branch_1_fun/ppermute | solution.py:36
  20.7 9.2 %copy-start.2 = (f32[256,512]{1,0:T(8,128)}, f32[256,512]{1,0:T(8,128)S(1)}, u32[]{:S(2)}) copy-start(f32[256,512]{1,0:T(8,128)S(1)} %get-tuple-element.451) | copy-start | bytes 1572868
  20.7 28.4 %collective-permute-start.19 = (bf16[96,2048]{1,0:T(8,128)(2,1)S(1)}, bf16[96,2048]{1,0:T(8,128)(2,1)}, u32[]{:S(2)}, u32[]{:S(2)}) collective-permute-start(bf16[96,2048]{1,0:T(8,128)(2,1)S(1)} %get-tuple-element.429), channel_id=1, source_target_pairs={{0,12},{4,8},{8,4},{12,0},{1,13},{5,9},{9,5},{13,1},{2,14},{6,10},... | collective-permute-start | bytes 1179656 | tf_op jit(solution)/shard_map/ppermute | solution.py:36
  20.8 42.4 %collective-permute-start.20 = (bf16[256,2048]{1,0:T(8,128)(2,1)}, bf16[256,2048]{1,0:T(8,128)(2,1)}, u32[]{:S(2)}, u32[]{:S(2)}) collective-permute-start(bf16[256,2048]{1,0:T(8,128)(2,1)} %act_ref.1), channel_id=1, source_target_pairs={{0,2},{1,3},{2,0},{3,1},{4,6},{5,7},{6,4},{7,5},{8,10},{9,11},{10,... | collective-permute-start | bytes 3145736 | tf_op jit(solution)/shard_map/ppermute | solution.py:36
  29.9 5.8 %collective-permute-start.1 = (bf16[160,128]{1,0:T(8,128)(2,1)S(1)}, bf16[160,128]{1,0:T(8,128)(2,1)S(1)}, u32[]{:S(2)}, u32[]{:S(2)}) collective-permute-start(bf16[160,128]{1,0:T(8,128)(2,1)S(1)} %get-tuple-element.315), channel_id=1, source_target_pairs={{0,1},{1,0},{2,3},{3,2},{4,5},{5,4},{6,7},{7,6},{8,9},{9,8},{10,11... | collective-permute-start | bytes 122888 | tf_op jit(solution)/shard_map/cond/branch_1_fun/ppermute | solution.py:36
  30.0 17.9 %collective-permute-start.2 = (bf16[160,128]{1,0:T(8,128)(2,1)S(1)}, bf16[160,128]{1,0:T(8,128)(2,1)S(1)}, u32[]{:S(2)}, u32[]{:S(2)}) collective-permute-start(bf16[160,128]{1,0:T(8,128)(2,1)S(1)} %get-tuple-element.316), channel_id=1, source_target_pairs={{0,2},{1,3},{2,0},{3,1},{4,6},{5,7},{6,4},{7,5},{8,10},{9,11},{10,... | collective-permute-start | bytes 122888 | tf_op jit(solution)/shard_map/cond/branch_1_fun/ppermute | solution.py:36
  31.6 16.4 %collective-permute-start.3 = (bf16[160,128]{1,0:T(8,128)(2,1)S(1)}, bf16[160,128]{1,0:T(8,128)(2,1)S(1)}, u32[]{:S(2)}, u32[]{:S(2)}) collective-permute-start(bf16[160,128]{1,0:T(8,128)(2,1)S(1)} %get-tuple-element.317), channel_id=1, source_target_pairs={{0,3},{1,2},{2,1},{3,0},{4,7},{5,6},{6,5},{7,4},{8,11},{9,10},{10,... | collective-permute-start | bytes 122888 | tf_op jit(solution)/shard_map/cond/branch_1_fun/ppermute | solution.py:36
  49.1 14.1 %copy-start.3 = (f32[256,512]{1,0:T(8,128)S(1)}, f32[256,512]{1,0:T(8,128)}, u32[]{:S(2)}) copy-start(f32[256,512]{1,0:T(8,128)} %copy-done.2) | copy-start | bytes 1572868
  52.2 1.9 %collective-permute-start.4 = (bf16[48,128]{1,0:T(8,128)(2,1)S(1)}, bf16[48,128]{1,0:T(8,128)(2,1)S(1)}, u32[]{:S(2)}, u32[]{:S(2)}) collective-permute-start(bf16[48,128]{1,0:T(8,128)(2,1)S(1)} %get-tuple-element.331), channel_id=1, source_target_pairs={{0,1},{1,0},{2,3},{3,2},{4,5},{5,4},{6,7},{7,6},{8,9},{9,8},{10,11... | collective-permute-start | bytes 36872 | tf_op jit(solution)/shard_map/cond/branch_1_fun/ppermute | solution.py:36
  52.5 3.7 %collective-permute-start.5 = (bf16[48,128]{1,0:T(8,128)(2,1)S(1)}, bf16[48,128]{1,0:T(8,128)(2,1)S(1)}, u32[]{:S(2)}, u32[]{:S(2)}) collective-permute-start(bf16[48,128]{1,0:T(8,128)(2,1)S(1)} %get-tuple-element.332), channel_id=1, source_target_pairs={{0,2},{1,3},{2,0},{3,1},{4,6},{5,7},{6,4},{7,5},{8,10},{9,11},{10,... | collective-permute-start | bytes 36872 | tf_op jit(solution)/shard_map/cond/branch_1_fun/ppermute | solution.py:36
  54.0 3.1 %collective-permute-start.6 = (bf16[48,128]{1,0:T(8,128)(2,1)S(1)}, bf16[48,128]{1,0:T(8,128)(2,1)S(1)}, u32[]{:S(2)}, u32[]{:S(2)}) collective-permute-start(bf16[48,128]{1,0:T(8,128)(2,1)S(1)} %get-tuple-element.333), channel_id=1, source_target_pairs={{0,3},{1,2},{2,1},{3,0},{4,7},{5,6},{6,5},{7,4},{8,11},{9,10},{10,... | collective-permute-start | bytes 36872 | tf_op jit(solution)/shard_map/cond/branch_1_fun/ppermute | solution.py:36
  58.0 12.2 %copy-start.4 = (s32[256,1]{0,1:T(1,128)S(1)}, s32[256,1]{0,1:T(1,128)}, u32[]{:S(2)}) copy-start(s32[256,1]{0,1:T(1,128)} %param.19) | copy-start | bytes 3076
  58.1 12.2 %copy-start.5 = (s32[64]{0:T(128)S(1)}, s32[64]{0:T(128)}, u32[]{:S(2)}) copy-start(s32[64]{0:T(128)} %param.20) | copy-start | bytes 772
  58.1 12.2 %collective-permute-start.22 = (bf16[112,512]{1,0:T(8,128)(2,1)}, bf16[112,512]{1,0:T(8,128)(2,1)S(1)}, u32[]{:S(2)}, u32[]{:S(2)}) collective-permute-start(bf16[112,512]{1,0:T(8,128)(2,1)} %get-tuple-element.447), channel_id=1, source_target_pairs={{0,4},{4,0},{8,12},{12,8},{1,5},{5,1},{9,13},{13,9},{2,6},{6,2},{1... | collective-permute-start | bytes 344072 | tf_op jit(solution)/shard_map/ppermute | solution.py:36
  58.7 11.6 %collective-permute-start.21 = (bf16[96,512]{1,0:T(8,128)(2,1)}, bf16[96,512]{1,0:T(8,128)(2,1)S(1)}, u32[]{:S(2)}, u32[]{:S(2)}) collective-permute-start(bf16[96,512]{1,0:T(8,128)(2,1)} %get-tuple-element.446), channel_id=1, source_target_pairs={{0,8},{4,12},{8,0},{12,4},{1,9},{5,13},{9,1},{13,5},{2,10},{6,14},... | collective-permute-start | bytes 294920 | tf_op jit(solution)/shard_map/ppermute | solution.py:36
  62.2 8.1 %collective-permute-start.23 = (bf16[96,512]{1,0:T(8,128)(2,1)S(1)}, bf16[96,512]{1,0:T(8,128)(2,1)S(1)}, u32[]{:S(2)}, u32[]{:S(2)}) collective-permute-start(bf16[96,512]{1,0:T(8,128)(2,1)S(1)} %get-tuple-element.445), channel_id=1, source_target_pairs={{0,12},{4,8},{8,4},{12,0},{1,13},{5,9},{9,5},{13,1},{2,14},{6,10},... | collective-permute-start | bytes 294920 | tf_op jit(solution)/shard_map/ppermute | solution.py:36
  63.2 2.9 %collective-permute-start.7 = (bf16[256,2048]{1,0:T(8,128)(2,1)}, bf16[256,2048]{1,0:T(8,128)(2,1)S(1)}, u32[]{:S(2)}, u32[]{:S(2)}) collective-permute-start(bf16[256,2048]{1,0:T(8,128)(2,1)} %get-tuple-element.337.refs_0_), channel_id=1, source_target_pairs={{0,1},{1,0},{2,3},{3,2},{4,5},{5,4},{6,7},{7,6},{8,9},{9,8},{10,11... | collective-permute-start | bytes 3145736 | tf_op jit(solution)/shard_map/cond/branch_1_fun/ppermute | solution.py:36

commit v2 on v1

--- a/solution.py
+++ b/solution.py
@@ -10,9 +10,8 @@
 KEY_VALUE_COLS = 1024
 LANES = 128
 MOST = 16
-NEAR = 2
-NEAR_ROWS = 112
-FAR_ROWS = 96
+OWN_ROWS = 112
+AWAY_ROWS = 96
 LATER_ROWS = 32
 VMEM = pltpu.VMEM
 MIB = 1 << 20
@@ -22,9 +21,7 @@
 
 def first_turn(wide_size, local_count):
     most = -(-(local_count * MOST + 1) // 32) * 32
-    blocks = [(k, 0, min(NEAR_ROWS if k < NEAR else FAR_ROWS, most)) for k in range(wide_size)]
-    half = wide_size // 2
-    return blocks[1 : half + 1][::-1], blocks[half + 1 :] + blocks[:1]
+    return [(k, 0, min(AWAY_ROWS if k else OWN_ROWS, most)) for k in reversed(range(wide_size))]
 
 
 def ends(blocks, wide_size):
@@ -188,28 +185,28 @@
     )(in_hbm(down_weight), in_hbm(up_weight))
 
 
-def down_kernel(count, cols, narrow_size, per_step, where_ref, *refs):
-    xs, weight_ref = refs[:count], refs[count]
-    flag_ref, ids_ref = refs[count + 1 : count + 3]
-    parts = refs[count + 3 : count + 3 + narrow_size]
-    (held_ref,) = refs[count + 3 + narrow_size :]
+def down_kernel(count, cols, narrow_size, per_step, where_ref, weight_ref, *refs):
+    xs, refs = refs[:count], refs[count:]
+    before, refs = (refs[:3], refs[3:]) if narrow_size else ((), refs)
+    flag_ref, ids_ref, *outs, held_ref = refs
     steps = weight_ref.shape[1] // (per_step * LANES)
 
-    offsets = [sum(x.shape[0] for x in xs[:n]) for n in range(count)]
-
     flag = jnp.zeros((1, LANES), f32)
-    for n in range(count):
-        rows = xs[n].shape[0]
-        held_ref[pl.ds(offsets[n], rows), :] = xs[n][...]
-        last = held_ref[pl.ds(offsets[n] + rows - 16, 16), :LANES].astype(f32)[15:]
+    ids = []
+    offset = 0
+    for x in xs:
+        rows = x.shape[0]
+        held_ref[pl.ds(offset, rows), :] = x[...]
+        last = x[pl.ds(rows - 16, 16), :LANES].astype(f32)[15:]
         flag = jnp.maximum(flag, last)
         turned = jnp.broadcast_to(last, (LANES, LANES)).T[:rows]
         keep = lax.broadcasted_iota(i32, (rows, LANES), 0) < rows - 1
-        ids_ref[pl.ds(offsets[n], rows), :] = jnp.where(keep, turned, 0.0)
+        ids.append(jnp.where(keep, turned, 0.0))
+        offset += rows
+    ids = jnp.concatenate(ids, axis=0)
     lane = lax.broadcasted_iota(i32, (1, LANES), 1)
-    flag_ref[0, 0] = jnp.max(jnp.where(lane == LANES - 1, flag, 0.0)).astype(i32)
-
-    ids = ids_ref[...]
+    flag = jnp.max(jnp.where(lane == LANES - 1, flag, 0.0)).astype(i32)
+
     total = jnp.zeros(ids.shape, f32)
     for c in range(steps):
         weights = weight_ref[:, c * per_step * LANES : (c + 1) * per_step * LANES]
@@ -218,6 +215,21 @@
             name = c * per_step + j + 1.0
             total = jnp.where(ids == name, found[:, j * LANES : (j + 1) * LANES], total)
 
+    if not narrow_size:
+        flag_ref[0, 0] = flag
+        ids_ref[...] = ids
+        outs[0][...] = total
+        return
+    if before:
+        flag = jnp.maximum(flag, before[0][0, 0])
+        ids = jnp.concatenate([before[1][...], ids], axis=0)
+        total = jnp.concatenate([before[2][...], total], axis=0)
+    flag_ref[0, 0] = flag
+    padding = jnp.zeros((ids_ref.shape[0] - ids.shape[0], LANES), f32)
+    if padding.shape[0]:
+        ids = jnp.concatenate([ids, padding], axis=0)
+        total = jnp.concatenate([total, padding], axis=0)
+    ids_ref[...] = ids
     half = total.shape[0] // 2
     rank = LANES // 2
     top, bottom = total[:half], total[half:]
@@ -226,29 +238,39 @@
     values = jnp.where(low, pltpu.roll(top, rank, 1), bottom)
     for j in range(narrow_size):
         start = jnp.bitwise_xor(where_ref[1], j) * cols
-        parts[j][...] = jnp.where(start >= KEY_VALUE_COLS, values, keys).astype(parts[j].dtype)
-
-
-def down(where, blocks, weight, cols, narrow_size, scale):
+        outs[j][...] = jnp.where(start >= KEY_VALUE_COLS, values, keys).astype(outs[j].dtype)
+
+
+def down(where, blocks, weight, cols, before, narrow_size, scale):
     features, width = weight.shape
-    rows = sum(b.shape[0] for b in blocks)
+    new_rows = sum(b.shape[0] for b in blocks)
     per_step = min(4, width // LANES)
     whole = pl.BlockSpec(memory_space=VMEM)
     scalar = pl.BlockSpec(memory_space=pltpu.SMEM)
+    if narrow_size:
+        rows = -(-(new_rows + before[1].shape[0]) // 32) * 32
+        sums = [((rows // 2, LANES), bf16 if j else f32) for j in range(narrow_size)]
+    else:
+        rows = new_rows
+        sums = [((rows, LANES), f32)]
     return pl.pallas_call(
         functools.partial(down_kernel, len(blocks), cols, narrow_size, per_step),
         out_shape=[
             jax.ShapeDtypeStruct((1, 1), i32),
             jax.ShapeDtypeStruct((rows, LANES), f32),
         ]
-        + [jax.ShapeDtypeStruct((rows // 2, LANES), bf16 if j else f32) for j in range(narrow_size)],
-        in_specs=[scalar] + [whole for _ in blocks] + [whole],
-        out_specs=[scalar, whole] + [whole for _ in range(narrow_size)],
-        scratch_shapes=[VMEM((rows, features), bf16)],
+        + [jax.ShapeDtypeStruct(*s) for s in sums],
+        in_specs=[scalar, whole]
+        + [whole for _ in blocks]
+        + ([scalar, whole, whole] if narrow_size else []),
+        out_specs=[scalar, whole] + [whole for _ in sums],
+        scratch_shapes=[VMEM((new_rows, features), bf16)],
         compiler_params=params(18),
-        cost_estimate=cost(2 * rows * features * width, 2 * features * (rows + width), scale),
+        cost_estimate=cost(
+            2 * new_rows * features * width, 2 * features * (new_rows + width), scale
+        ),
         name="down_maps",
-    )(where, *blocks, weight)
+    )(where, weight, *blocks, *(before if narrow_size else []))
 
 
 def up_kernel(narrow_size, ids_ref, *refs):
@@ -366,15 +388,9 @@
     )(base_out, place, *corrections)
 
 
-def raise_parts(ids, parts, up_weight, counts):
-    parts = [swap(p, "narrow", j) if j else p for j, p in enumerate(parts)]
-    return up(ids, parts, up_weight, counts)
-
-
-def answers_for(where, blocks, maps, narrow_size):
-    down_weight, up_weight = maps
-    more, ids, *parts = down(where, blocks, down_weight, up_weight.shape[1], narrow_size, 0.001)
-    return raise_parts(ids, parts, up_weight, [b.shape[0] for b in blocks]), more
+def raise_sums(ids, sums, up_weight, counts):
+    sums = [swap(part, "narrow", j) if j else part for j, part in enumerate(sums)]
+    return up(ids, sums, up_weight, counts)
 
 
 def later_turn(turn, axes, total, done, tenant, slot, activations, down_weight, up_weight):
@@ -393,7 +409,11 @@
         LATER_ROWS - 1,
     )
     got = [swap(b, "wide", k) if k else b for k, b in enumerate(sent)]
-    outs, more = answers_for(where, got, stage(down_weight, up_weight), narrow_size)
+    cols = up_weight.shape[1]
+    down_weight, up_weight = stage(down_weight, up_weight)
+    before = down(where, got[:1], down_weight, cols, None, 0, 0.001)
+    more, ids, *sums = down(where, got[1:], down_weight, cols, before, narrow_size, 0.001)
+    outs = raise_sums(ids, sums, up_weight, [b.shape[0] for b in got])
     answers = [swap(b, "wide", k) if k else b for k, b in enumerate(outs)]
     return join(total, place, answers, f32), more[0, 0]
 
@@ -416,13 +436,11 @@
     up_weight = adapter_up_weight.reshape(-1, adapter_up_weight.shape[-1])
 
     cols = up_weight.shape[1]
-    first, second = first_turn(wide_size, local_count)
-    layout = first + second
+    layout = first_turn(wide_size, local_count)
+    own = len(layout) - 1
     routed = (local_count, wide_size, layout)
-    begun, place, *sent = pack(
-        where, tenant, slot, activations, *routed, (0, len(first)), 0
-    )
-    got = [swap(b, "wide", k) for (k, _, _), b in zip(first, sent)]
+    begun, place, *sent = pack(where, tenant, slot, activations, *routed, (0, own), 0)
+    got = [swap(b, "wide", k) for (k, _, _), b in zip(layout, sent)]
     half = narrow_size // 2
 
     def step(work, *operands):
@@ -440,35 +458,28 @@
             bit //= 2
         return [acts[j] for j in sorted(acts)]
 
-    def work_before(tenant, slot, activations, shared_weight, maps):
-        _, _, *sent = pack(
-            where, tenant, slot, activations, *routed, (len(first), len(layout)), 0
-        )
-        return sent, base(where, spread(activations), 0, shared_weight, None), stage(*maps)
-
-    def work_on_first(ids, parts, up_weight, maps):
-        counts = [count for _, _, count in [*first, layout[-1]]]
-        return raise_parts(ids, parts, up_weight, counts), stage(*maps)
-
-    def work_on_second(blocks, maps):
-        return answers_for(where, blocks, maps, narrow_size)
+    def pack_own(tenant, slot, activations):
+        return pack(where, tenant, slot, activations, *routed, (own, own + 1), 0)[2]
+
+    def work_before(activations, shared_weight, maps):
+        return base(where, spread(activations), 0, shared_weight, None), stage(*maps)
 
     def work_after(across, shared_weight, base_out):
         return base(where, spread(across), half, shared_weight, base_out)
 
     shared_weight, maps = after_all((shared_weight, (adapter_down_weight, up_weight)), *sent)
-    sent, base_out, staged = step(work_before, tenant, slot, activations, shared_weight, maps)
-    across = swap(after(activations, base_out), "narrow", half) if half else None
-    late = [swap(b, "wide", k) for (k, _, _), b in zip(second, sent[:-1])]
-    more, ids, *parts = down(
-        where, [*got, sent[-1]], staged[0], up_weight.shape[1], narrow_size, 20
-    )
-    outs, staged = step(work_on_first, ids, parts, staged[1], maps)
-    if late:
-        late_outs, late_more = step(work_on_second, after_all(late, *outs), staged)
-        more = jnp.maximum(more, late_more)
-        outs = after_all(outs, *late_outs)
-        outs = [*outs[:-1], *late_outs, outs[-1]]
+    own_block = step(pack_own, tenant, slot, activations)
+    across = swap(after(activations, own_block), "narrow", half) if half else None
+    base_out, (down_beside, up_beside) = step(
+        work_before, *after_all((activations, shared_weight, maps), own_block)
+    )
+    before = down(where, [got[-1], after(own_block, base_out)], down_beside, cols, None, 0, 0.001)
+    more, ids, *sums = down(
+        where, after_all(got[:-1], *before), down_beside, cols, before, narrow_size, 20
+    )
+    counts = [layout[n][2] for n in (own - 1, own, *range(own - 1))]
+    outs = raise_sums(ids, sums, up_beside, counts)
+    outs = [*outs[2:], *outs[:2]]
     answers = [swap(b, "wide", k) if k else b for (k, _, _), b in zip(layout, outs)]
     if half:
         base_out = step(work_after, *after_all((across, shared_weight, base_out), *outs))

time: 71.9 us -> 66.6 us (0.926)
  Pallas kernels: 31.5 us -> 26.1 us
  waiting for transfers between devices: 21.7 us -> 24.5 us
  starting transfers between devices: 15.9 us -> 13.7 us
    pallas_call x2 -> x1, Pallas kernels: 7.73 us -> 3.86 us  [stage(): pl.pallas_call(stage_kernel, out_shape=[pltpu.VMEM((features, adapters *...]
    ppermute x15 -> x12, waiting for transfers between devices: 21.7 us -> 24.5 us  [swap(): return lax.ppermute(x, axis, [(i, i ^ k) for i in range(size)])]
    ppermute x15 -> x12, starting transfers between devices: 15.9 us -> 13.7 us  [swap(): return lax.ppermute(x, axis, [(i, i ^ k) for i in range(size)])]
    pallas_call x2 -> x1, Pallas kernels: 1.53 us -> 0.65 us  [up(): pl.pallas_call(functools.partial(up_kernel, len(parts)), out_shape=[jax.S...]
    pallas_call x2, Pallas kernels: 7.06 us -> 6.31 us  [down(): pl.pallas_call(functools.partial(down_kernel, len(blocks), cols, narrow_s...]
  transfers between devices with their start and end apart: 15 -> 12, of which waited for: 7 -> 5; matrix products, arithmetic and copies ran while one was open for 0% -> 0% of each run, Pallas kernels for 38% -> 32%
where the time goes in v2:
time: 66.6 us; the launch traced here: 66.4 us
  Pallas kernels  26.1 us (39%)
  waiting for transfers between devices  24.5 us (37%)
  starting transfers between devices  13.7 us (21%)
  between operations  1.65 us (2%)
    ppermute x12, waiting for transfers between devices, swap(): return lax.ppermute(x, axis, [(i, i ^ k) for i in range(size)])  24.5 us
    ppermute x12, starting transfers between devices, swap(): return lax.ppermute(x, axis, [(i, i ^ k) for i in range(size)])  13.7 us
    pallas_call x2, Pallas kernels, base(): pl.pallas_call(functools.partial(base_kernel, count), grid_spec=pltpu.Pre...  7.74 us
    pallas_call x2, Pallas kernels, pack(): pl.pallas_call(functools.partial(pack_kernel, local_count, wide_size, lay...  6.53 us
    pallas_call x2, Pallas kernels, down(): pl.pallas_call(functools.partial(down_kernel, len(blocks), cols, narrow_s...  6.31 us
    pallas_call x1, Pallas kernels, stage(): pl.pallas_call(stage_kernel, out_shape=[pltpu.VMEM((features, adapters *...  3.86 us
  transfers between devices with their start and end apart: 12, of which 5 were waited for; matrix products, arithmetic and copies ran while one was open for 0% of the time, Pallas kernels for 32%

profile of v2, /device:TPU:0, one launch (start us, length us, event | category | flops | bytes accessed | tf_op | source)
XLA Modules:
  0.0 66.4 jit_solution(3868166109882727557)
XLA Ops:
  0.1 3.5 %pack_rows.8 = (s32[1,1]{1,0:T(1,128)}, f32[256,128]{1,0:T(8,128)}, bf16[96,2048]{1,0:T(8,128)(2,1)S(1)}, bf16[96,2048]{1,0:T(8,128)(2,1)S(1)}, bf16[96,2048]{1,0:T(8,128)(2,1)}) custom-call(s32[3]{0:T(128)S(1)} %pad_add_fusion.1.where_ref, s32[1,256]{1,0:T(1,128)} %bitcast.21, s32[1,64]{1,0:T(1,128)} %bitcast.24, bf16[256,2048]{1,0:T(8,128)(2,1)} %act_ref.1), custom_call_target="tpu_custom_call" | custom-call | flops 301989 | bytes 2228 | tf_op jit(solution)/shard_map/pack_rows/pallas_call | solution.py:139
  3.6 3.1 %collective-permute-start.13 = (bf16[96,2048]{1,0:T(8,128)(2,1)}, bf16[96,2048]{1,0:T(8,128)(2,1)S(1)}, u32[]{:S(2)}, u32[]{:S(2)}) collective-permute-start(bf16[96,2048]{1,0:T(8,128)(2,1)} %get-tuple-element.389), channel_id=1, source_target_pairs={{0,4},{4,0},{8,12},{12,8},{1,5},{5,1},{9,13},{13,9},{2,6},{6,2},{1... | collective-permute-start | bytes 1179656 | tf_op jit(solution)/shard_map/ppermute | solution.py:33
  6.7 2.5 %collective-permute-start.11 = (bf16[96,2048]{1,0:T(8,128)(2,1)S(1)}, bf16[96,2048]{1,0:T(8,128)(2,1)S(1)}, u32[]{:S(2)}, u32[]{:S(2)}) collective-permute-start(bf16[96,2048]{1,0:T(8,128)(2,1)S(1)} %get-tuple-element.387), channel_id=1, source_target_pairs={{0,12},{4,8},{8,4},{12,0},{1,13},{5,9},{9,5},{13,1},{2,14},{6,10},... | collective-permute-start | bytes 1179656 | tf_op jit(solution)/shard_map/ppermute | solution.py:33
  9.9 3.0 %conditional.4 = (bf16[112,2048]{1,0:T(8,128)(2,1)S(1)}) conditional(s32[]{:T(128)} %bitcast.8, () %tuple.61, (s32[3]{0:T(128)S(1)}, s32[1,256]{1,0:T(1,128)}, s32[1,64]{1,0:T(1,128)}, bf16[256,2048]{1,0:T(8,128)(2,1)}) %tuple.101), branch_computations={%region_0.0_spmd, %region_1.0_spmd} | conditional | flops 117440 | bytes 458762 | solution.py:452
  9.9 3.0 %pack_rows.7 = (s32[1,1]{1,0:T(1,128)}, f32[256,128]{1,0:T(8,128)}, bf16[112,2048]{1,0:T(8,128)(2,1)S(1)}) custom-call(s32[3]{0:T(128)S(1)} %get-tuple-element.285.where_ref, s32[1,256]{1,0:T(1,128)} %get-tuple-element.286.tenant_ref, s32[1,64]{1,0:T(1,128)} %get-tuple-element.287.slot_ref, bf16[256,2048]{1,0:T(8,128)(2,1)} %get-tuple-element.288.act_ref), custom_call_target="tpu_custom_call" | custom-call | flops 117440 | bytes 1507 | tf_op jit(solution)/shard_map/cond/branch_1_fun/pack_rows/pallas_call | solution.py:139
  13.0 1.5 %collective-permute-start.14 = (bf16[256,2048]{1,0:T(8,128)(2,1)}, bf16[256,2048]{1,0:T(8,128)(2,1)}, u32[]{:S(2)}, u32[]{:S(2)}) collective-permute-start(bf16[256,2048]{1,0:T(8,128)(2,1)} %act_ref.1), channel_id=1, source_target_pairs={{0,2},{1,3},{2,0},{3,1},{4,6},{5,7},{6,4},{7,5},{8,10},{9,11},{10,... | collective-permute-start | bytes 3145736 | tf_op jit(solution)/shard_map/ppermute | solution.py:33
  14.5 7.8 %conditional.5 = (f32[256,512]{1,0:T(8,128)S(1)}, bf16[2048,2048]{1,0:T(8,128)(2,1)S(1)}, bf16[1024,512]{1,0:T(8,128)(2,1)S(1)}) conditional(s32[]{:T(128)} %bitcast.8, () %tuple.59, (bf16[256,2048]{1,0:T(8,128)(2,1)}, s32[3]{0:T(128)S(1)}, bf16[8192,512]{1,0:T(8,128)(2,1)}, bf16[16,2048,128]{2,1,0:T(8,128)(2,1)}, bf16[1024,512]{1,0:T(8,128)(2,1)}) %tuple.95), branch_computations={%region_2.0_spmd, %region_3.0_spmd} | conditional | flops 1073741 | bytes 9961504 | solution.py:452
  14.5 3.9 %stage_maps.4 = (bf16[2048,2048]{1,0:T(8,128)(2,1)S(1)}, bf16[1024,512]{1,0:T(8,128)(2,1)S(1)}) custom-call(bf16[16,2048,128]{2,1,0:T(8,128)(2,1)} %get-tuple-element.293.down_ref, bf16[1024,512]{1,0:T(8,128)(2,1)} %get-tuple-element.294.up_ref), custom_call_target="tpu_custom_call" | custom-call | tf_op jit(solution)/shard_map/cond/branch_1_fun/stage_maps/pallas_call | solution.py:173
  18.4 3.9 %shared_projection.2 = f32[256,512]{1,0:T(8,128)S(1)} custom-call(s32[3]{0:T(128)S(1)} %get-tuple-element.290.where_ref, bf16[256,2048]{1,0:T(8,128)(2,1)} %get-tuple-element.291.refs_0_, bf16[256,2048]{1,0:T(8,128)(2,1)S(1)} %collective-permute-done.refs_1_, bf16[8192,512]{1,0:T(8,128)(2,1)} %get-tuple-element.292.refs_2_), custom_call_target="tpu_custom_call" | custom-call | flops 1073741 | bytes 6291 | tf_op jit(solution)/shard_map/cond/branch_1_fun/shared_projection/pallas_call | solution.py:334
  22.3 2.9 %down_maps.12 = (s32[1,1]{1,0:T(1,128)}, f32[208,128]{1,0:T(8,128)S(1)}, f32[208,128]{1,0:T(8,128)S(1)}) custom-call(s32[3]{0:T(128)S(1)} %pad_add_fusion.1.where_ref, bf16[2048,2048]{1,0:T(8,128)(2,1)S(1)} %get-tuple-element.397.weight_ref, bf16[96,2048]{1,0:T(8,128)(2,1)S(1)} %collective-permute-done.13.refs_0_, ...), custom_call_target="tpu_custom_call" | custom-call | flops 1744830 | bytes 9240 | tf_op jit(solution)/shard_map/down_maps/pallas_call | solution.py:256
  25.2 2.7 %collective-permute-done.11.refs_0_ = bf16[96,2048]{1,0:T(8,128)(2,1)S(1)} collective-permute-done((bf16[96,2048]{1,0:T(8,128)(2,1)S(1)}, bf16[96,2048]{1,0:T(8,128)(2,1)S(1)}, u32[]{:S(2)}, u32[]{:S(2)}) %collective-permute-start.11) | collective-permute-done | bytes 393248 | tf_op jit(solution)/shard_map/ppermute | solution.py:33
  27.9 15.5 %collective-permute-done.12.refs_1_ = bf16[96,2048]{1,0:T(8,128)(2,1)S(1)} collective-permute-done((bf16[96,2048]{1,0:T(8,128)(2,1)S(1)}, bf16[96,2048]{1,0:T(8,128)(2,1)S(1)}, u32[]{:S(2)}, u32[]{:S(2)}) %collective-permute-start.12) | collective-permute-done | bytes 393248 | tf_op jit(solution)/shard_map/ppermute | solution.py:33
  43.4 3.4 %down_maps.13 = (s32[1,1]{1,0:T(1,128)}, f32[416,128]{1,0:T(8,128)S(1)}, f32[208,128]{1,0:T(8,128)S(1)}, bf16[208,128]{1,0:T(8,128)(2,1)S(1)}, bf16[208,128]{1,0...) custom-call(s32[3]{0:T(128)S(1)} %pad_add_fusion.1.where_ref, bf16[2048,2048]{1,0:T(8,128)(2,1)S(1)} %get-tuple-element.397.weight_ref, ...), custom_call_target="tpu_custom_call" | custom-call | flops 32212254720 | bytes 183500800 | tf_op jit(solution)/shard_map/down_maps/pallas_call | solution.py:256
  46.9 1.6 %collective-permute-start.16 = (bf16[208,128]{1,0:T(8,128)(2,1)S(1)}, bf16[208,128]{1,0:T(8,128)(2,1)S(1)}, u32[]{:S(2)}, u32[]{:S(2)}) collective-permute-start(bf16[208,128]{1,0:T(8,128)(2,1)S(1)} %get-tuple-element.410), channel_id=1, source_target_pairs={{0,2},{1,3},{2,0},{3,1},{4,6},{5,7},{6,4},{7,5},{8,10},{9,11},{10,... | collective-permute-start | bytes 159752 | tf_op jit(solution)/shard_map/ppermute | solution.py:33
  48.8 2.4 %collective-permute-done.16.refs_2_ = bf16[208,128]{1,0:T(8,128)(2,1)S(1)} collective-permute-done((bf16[208,128]{1,0:T(8,128)(2,1)S(1)}, bf16[208,128]{1,0:T(8,128)(2,1)S(1)}, u32[]{:S(2)}, u32[]{:S(2)}) %collective-permute-start.16) | collective-permute-done | bytes 53280 | tf_op jit(solution)/shard_map/ppermute | solution.py:33
  51.2 1.1 %collective-permute-done.17.refs_3_ = bf16[208,128]{1,0:T(8,128)(2,1)S(1)} collective-permute-done((bf16[208,128]{1,0:T(8,128)(2,1)S(1)}, bf16[208,128]{1,0:T(8,128)(2,1)S(1)}, u32[]{:S(2)}, u32[]{:S(2)}) %collective-permute-start.17) | collective-permute-done | bytes 53280 | tf_op jit(solution)/shard_map/ppermute | solution.py:33
  52.3 0.6 up_maps.6
  52.9 2.7 %collective-permute-start.18 = (bf16[96,512]{1,0:T(8,128)(2,1)S(1)}, bf16[96,512]{1,0:T(8,128)(2,1)S(1)}, u32[]{:S(2)}, u32[]{:S(2)}) collective-permute-start(bf16[96,512]{1,0:T(8,128)(2,1)S(1)} %get-tuple-element.413), channel_id=1, source_target_pairs={{0,12},{4,8},{8,4},{12,0},{1,13},{5,9},{9,5},{13,1},{2,14},{6,10},... | collective-permute-start | bytes 294920 | tf_op jit(solution)/shard_map/ppermute | solution.py:33
  55.6 1.7 %collective-permute-start.20 = (bf16[96,512]{1,0:T(8,128)(2,1)S(1)}, bf16[96,512]{1,0:T(8,128)(2,1)S(1)}, u32[]{:S(2)}, u32[]{:S(2)}) collective-permute-start(bf16[96,512]{1,0:T(8,128)(2,1)S(1)} %get-tuple-element.415), channel_id=1, source_target_pairs={{0,4},{4,0},{8,12},{12,8},{1,5},{5,1},{9,13},{13,9},{2,6},{6,2},{1... | collective-permute-start | bytes 294920 | tf_op jit(solution)/shard_map/ppermute | solution.py:33
  58.1 6.8 %conditional.6 = (f32[256,512]{1,0:T(8,128)S(1)}) conditional(s32[]{:T(128)} %bitcast.8, () %tuple.67, (bf16[256,2048]{1,0:T(8,128)(2,1)}, s32[3]{0:T(128)S(1)}, bf16[8192,512]{1,0:T(8,128)(2,1)}, f32[256,512]{1,0:T(8,128)S(1)}) %tuple.70), branch_computations={%region_4.0_spmd, %region_5.0_spmd} | conditional | flops 1073741 | bytes 4200643 | solution.py:452
  58.2 2.9 %collective-permute-done.1.refs_1_ = bf16[256,2048]{1,0:T(8,128)(2,1)S(1)} collective-permute-done((bf16[256,2048]{1,0:T(8,128)(2,1)}, bf16[256,2048]{1,0:T(8,128)(2,1)S(1)}, u32[]{:S(2)}, u32[]{:S(2)}) %collective-permute-start.1) | collective-permute-done | bytes 1048608 | tf_op jit(solution)/shard_map/cond/branch_1_fun/ppermute | solution.py:33
  61.0 3.9 %shared_projection.3 = f32[256,512]{1,0:T(8,128)S(1)} custom-call(s32[3]{0:T(128)S(1)} %get-tuple-element.297.where_ref, bf16[256,2048]{1,0:T(8,128)(2,1)} %get-tuple-element.298.refs_0_, bf16[256,2048]{1,0:T(8,128)(2,1)S(1)} %collective-permute-done.1.refs_1_, bf16[8192,512]{1,0:T(8,128)(2,1)} %get-tuple-element.299.refs_2_, ...), custom_call_target="tpu_custom_call" | custom-call | flops 1073741 | bytes 6291 | tf_op jit(solution)/shard_map/cond/branch_1_fun/shared_projection/pallas_call | solution.py:334
  65.0 1.2 %conditional.7 = (bf16[256,512]{1,0:T(8,128)(2,1)}) conditional(s32[]{:T(128)} %bitcast.10, (f32[256,512]{1,0:T(8,128)S(1)}, f32[256,128]{1,0:T(8,128)S(1)}, bf16[96,512]{1,0:T(8,128)(2,1)S(1)}, bf16[96,512]{1,0:T(8,128)(2,1)S(1)}, bf16[96,512]{1,0:T(8,128)(2,1)S(1)}, /*index=5*/bf16[112,512]{1,0:T(8,128)(2,1)S(1)}) %tuple.97, ...), branch_computations={%region_6.0_spmd, %region_7.0_spmd} | conditional | flops 1611666 | bytes 73226696 | solution.py:502
  65.0 1.0 %join_corrections.7 = bf16[256,512]{1,0:T(8,128)(2,1)} custom-call(f32[256,512]{1,0:T(8,128)S(1)} %get-tuple-element.301.base_ref, f32[256,128]{1,0:T(8,128)S(1)} %get-tuple-element.302.place_ref, bf16[96,512]{1,0:T(8,128)(2,1)S(1)} %get-tuple-element.303.refs_0_, bf16[96,512]{1,0:T(8,128)(2,1)S(1)} %get-tuple-element.304.refs_1_, ...), custom_call_target="tpu_custom_call" | custom-call | flops 104857 | bytes 1196 | tf_op jit(solution)/shard_map/cond/branch_0_fun/join_corrections/pallas_call | solution.py:379
  (20 shorter events, 0.7 us)
Async XLA Ops:
  3.6 18.7 %collective-permute-start.13 = (bf16[96,2048]{1,0:T(8,128)(2,1)}, bf16[96,2048]{1,0:T(8,128)(2,1)S(1)}, u32[]{:S(2)}, u32[]{:S(2)}) collective-permute-start(bf16[96,2048]{1,0:T(8,128)(2,1)} %get-tuple-element.389), channel_id=1, source_target_pairs={{0,4},{4,0},{8,12},{12,8},{1,5},{5,1},{9,13},{13,9},{2,6},{6,2},{1... | collective-permute-start | bytes 1179656 | tf_op jit(solution)/shard_map/ppermute | solution.py:33
  6.7 21.2 %collective-permute-start.11 = (bf16[96,2048]{1,0:T(8,128)(2,1)S(1)}, bf16[96,2048]{1,0:T(8,128)(2,1)S(1)}, u32[]{:S(2)}, u32[]{:S(2)}) collective-permute-start(bf16[96,2048]{1,0:T(8,128)(2,1)S(1)} %get-tuple-element.387), channel_id=1, source_target_pairs={{0,12},{4,8},{8,4},{12,0},{1,13},{5,9},{9,5},{13,1},{2,14},{6,10},... | collective-permute-start | bytes 1179656 | tf_op jit(solution)/shard_map/ppermute | solution.py:33
  9.2 34.2 %collective-permute-start.12 = (bf16[96,2048]{1,0:T(8,128)(2,1)S(1)}, bf16[96,2048]{1,0:T(8,128)(2,1)S(1)}, u32[]{:S(2)}, u32[]{:S(2)}) collective-permute-start(bf16[96,2048]{1,0:T(8,128)(2,1)S(1)} %get-tuple-element.388), channel_id=1, source_target_pairs={{0,8},{4,12},{8,0},{12,4},{1,9},{5,13},{9,1},{13,5},{2,10},{6,14},... | collective-permute-start | bytes 1179656 | tf_op jit(solution)/shard_map/ppermute | solution.py:33
  13.0 45.1 %collective-permute-start.14 = (bf16[256,2048]{1,0:T(8,128)(2,1)}, bf16[256,2048]{1,0:T(8,128)(2,1)}, u32[]{:S(2)}, u32[]{:S(2)}) collective-permute-start(bf16[256,2048]{1,0:T(8,128)(2,1)} %act_ref.1), channel_id=1, source_target_pairs={{0,2},{1,3},{2,0},{3,1},{4,6},{5,7},{6,4},{7,5},{8,10},{9,11},{10,... | collective-permute-start | bytes 3145736 | tf_op jit(solution)/shard_map/ppermute | solution.py:33
  14.5 3.9 %collective-permute-start = (bf16[256,2048]{1,0:T(8,128)(2,1)}, bf16[256,2048]{1,0:T(8,128)(2,1)S(1)}, u32[]{:S(2)}, u32[]{:S(2)}) collective-permute-start(bf16[256,2048]{1,0:T(8,128)(2,1)} %get-tuple-element.291.refs_0_), channel_id=1, source_target_pairs={{0,1},{1,0},{2,3},{3,2},{4,5},{5,4},{6,7},{7,6},{8,9},{9,8},{10,11... | collective-permute-start | bytes 3145736 | tf_op jit(solution)/shard_map/cond/branch_1_fun/ppermute | solution.py:33
  46.8 18.1 %copy-start.3 = (f32[256,128]{1,0:T(8,128)S(1)}, f32[256,128]{1,0:T(8,128)}, u32[]{:S(2)}) copy-start(f32[256,128]{1,0:T(8,128)} %get-tuple-element.420) | copy-start | bytes 393220
  46.8 18.1 %copy-start.4 = (s32[256,1]{0,1:T(1,128)S(1)}, s32[256,1]{0,1:T(1,128)}, u32[]{:S(2)}) copy-start(s32[256,1]{0,1:T(1,128)} %param.17) | copy-start | bytes 3076
  46.8 18.1 %copy-start.5 = (s32[64]{0:T(128)S(1)}, s32[64]{0:T(128)}, u32[]{:S(2)}) copy-start(s32[64]{0:T(128)} %param.18) | copy-start | bytes 772
  46.8 1.9 %collective-permute-start.15 = (bf16[208,128]{1,0:T(8,128)(2,1)S(1)}, bf16[208,128]{1,0:T(8,128)(2,1)S(1)}, u32[]{:S(2)}, u32[]{:S(2)}) collective-permute-start(bf16[208,128]{1,0:T(8,128)(2,1)S(1)} %get-tuple-element.409), channel_id=1, source_target_pairs={{0,1},{1,0},{2,3},{3,2},{4,5},{5,4},{6,7},{7,6},{8,9},{9,8},{10,11... | collective-permute-start | bytes 159752 | tf_op jit(solution)/shard_map/ppermute | solution.py:33
  46.9 4.2 %collective-permute-start.16 = (bf16[208,128]{1,0:T(8,128)(2,1)S(1)}, bf16[208,128]{1,0:T(8,128)(2,1)S(1)}, u32[]{:S(2)}, u32[]{:S(2)}) collective-permute-start(bf16[208,128]{1,0:T(8,128)(2,1)S(1)} %get-tuple-element.410), channel_id=1, source_target_pairs={{0,2},{1,3},{2,0},{3,1},{4,6},{5,7},{6,4},{7,5},{8,10},{9,11},{10,... | collective-permute-start | bytes 159752 | tf_op jit(solution)/shard_map/ppermute | solution.py:33
  48.5 3.8 %collective-permute-start.17 = (bf16[208,128]{1,0:T(8,128)(2,1)S(1)}, bf16[208,128]{1,0:T(8,128)(2,1)S(1)}, u32[]{:S(2)}, u32[]{:S(2)}) collective-permute-start(bf16[208,128]{1,0:T(8,128)(2,1)S(1)} %get-tuple-element.411), channel_id=1, source_target_pairs={{0,3},{1,2},{2,1},{3,0},{4,7},{5,6},{6,5},{7,4},{8,11},{9,10},{10,... | collective-permute-start | bytes 159752 | tf_op jit(solution)/shard_map/ppermute | solution.py:33
  52.9 12.0 %collective-permute-start.18 = (bf16[96,512]{1,0:T(8,128)(2,1)S(1)}, bf16[96,512]{1,0:T(8,128)(2,1)S(1)}, u32[]{:S(2)}, u32[]{:S(2)}) collective-permute-start(bf16[96,512]{1,0:T(8,128)(2,1)S(1)} %get-tuple-element.413), channel_id=1, source_target_pairs={{0,12},{4,8},{8,4},{12,0},{1,13},{5,9},{9,5},{13,1},{2,14},{6,10},... | collective-permute-start | bytes 294920 | tf_op jit(solution)/shard_map/ppermute | solution.py:33
  55.6 9.3 %collective-permute-start.19 = (bf16[96,512]{1,0:T(8,128)(2,1)S(1)}, bf16[96,512]{1,0:T(8,128)(2,1)S(1)}, u32[]{:S(2)}, u32[]{:S(2)}) collective-permute-start(bf16[96,512]{1,0:T(8,128)(2,1)S(1)} %get-tuple-element.414), channel_id=1, source_target_pairs={{0,8},{4,12},{8,0},{12,4},{1,9},{5,13},{9,1},{13,5},{2,10},{6,14},... | collective-permute-start | bytes 294920 | tf_op jit(solution)/shard_map/ppermute | solution.py:33
  55.6 9.3 %collective-permute-start.20 = (bf16[96,512]{1,0:T(8,128)(2,1)S(1)}, bf16[96,512]{1,0:T(8,128)(2,1)S(1)}, u32[]{:S(2)}, u32[]{:S(2)}) collective-permute-start(bf16[96,512]{1,0:T(8,128)(2,1)S(1)} %get-tuple-element.415), channel_id=1, source_target_pairs={{0,4},{4,0},{8,12},{12,8},{1,5},{5,1},{9,13},{13,9},{2,6},{6,2},{1... | collective-permute-start | bytes 294920 | tf_op jit(solution)/shard_map/ppermute | solution.py:33
  58.1 2.9 %collective-permute-start.1 = (bf16[256,2048]{1,0:T(8,128)(2,1)}, bf16[256,2048]{1,0:T(8,128)(2,1)S(1)}, u32[]{:S(2)}, u32[]{:S(2)}) collective-permute-start(bf16[256,2048]{1,0:T(8,128)(2,1)} %get-tuple-element.298.refs_0_), channel_id=1, source_target_pairs={{0,1},{1,0},{2,3},{3,2},{4,5},{5,4},{6,7},{7,6},{8,9},{9,8},{10,11... | collective-permute-start | bytes 3145736 | tf_op jit(solution)/shard_map/cond/branch_1_fun/ppermute | solution.py:33
